TPU v7x, 256 devices: a whole 4x4x8 slice. The times are simulated.
256 devices in a mesh: frame: 8 (over z), space: 4 (over y_lo, core), tensor: 8 (over y_hi, x).
Axes of the slice: x: 4, y: 4 (y_hi: 2, y_lo: 2; y = y_hi * 2 + y_lo), z: 8, core: 2. Of those that a mesh axis runs over, the one named last changes fastest.
Arguments:
- inputs: bfloat16 [2, 16, 576, 2048], P(None, 'frame', 'space'), may hold values from -6 to 6
- upstream: bfloat16 [2, 16, 576, 2048], P(None, 'frame', 'space'), may hold values from -6 to 6
- action_ids: int32 [2, 16], P(None, 'frame'), may hold values from 0 to 7
- frame_time: int32 [2, 16], replicated, may hold values from 0 to 15, each once within a row
- action_table: float32 [8, 2048], replicated, may hold values from -3 to 3
- gain: float32 [2048], replicated, may hold values from 0.5 to 1.5
- w_qkv: bfloat16 [2048, 3, 2048], P(('frame', 'space'), None, 'tensor'), may hold values from -1 to 1
- w_out: bfloat16 [2048, 2048], P(('frame', 'space'), 'tensor'), may hold values from -0.125 to 0.125
Outputs:
- grad_inputs: bfloat16 [2, 16, 576, 2048], P(None, 'frame', 'space')
- grad_qkv: float32 [2048, 3, 2048], P(('frame', 'space'), None, 'tensor')
- grad_out_proj: float32 [2048, 2048], P(('frame', 'space'), 'tensor')
- grad_gain: float32 [2048], replicated
- grad_actions: float32 [8, 2048], replicated
All inputs are finite; a program needn't handle non-finite values.
Results may differ from a plain program's by a relative error of at most 0.018.
The roundings to bfloat16 on the way count: a program that leaves them out, or rounds other values in their place, can miss the bound.
Values may be sent and summed in bfloat16 or wider, within the bound.
A program may use at most 128 MiB of HBM per device.

v0:
```python
import math

import jax
import jax.numpy as jnp
from jax import lax
from jax.sharding import PartitionSpec as P

HEAD = 128


NORM_EPSILON = 1e-06


def normalize(inputs, action_ids, action_table, gain):
    action_count = action_table.shape[0]
    onehot = (action_ids[..., None] == jnp.arange(action_count, dtype=jnp.int32)).astype(
        jnp.float32
    )
    embedded = jnp.einsum("bfa,ad->bfd", onehot, action_table, precision=lax.Precision.HIGHEST)
    hidden = inputs.astype(jnp.float32) + embedded[:, :, None, :]
    inverse = lax.rsqrt(jnp.mean(hidden * hidden, -1, keepdims=True) + NORM_EPSILON)
    unit_rows = hidden * inverse
    normed = (unit_rows * gain).astype(jnp.bfloat16)
    return (onehot, inverse, unit_rows, normed)


def temporal_attention(merged_qkv, grad_heads, frame_time, head_size):
    batch_count, frame_count, space_count, channel_count = merged_qkv.shape
    head_width = channel_count // 3
    head_count = head_width // head_size
    split_parts = merged_qkv.reshape(
        batch_count, frame_count, space_count, 3, head_count, head_size
    ).astype(jnp.float32)
    queries = split_parts[:, :, :, 0]
    key_rows = split_parts[:, :, :, 1]
    value_rows = split_parts[:, :, :, 2]
    score_scale = 1.0 / math.sqrt(head_size)
    scores = jnp.einsum("bqshd,bkshd->bshqk", queries, key_rows) * score_scale
    allowed = frame_time[:, None, None, None, :] <= frame_time[:, None, None, :, None]
    scores = jnp.where(allowed, scores, -1e30)
    row_maxima = jnp.max(scores, -1, keepdims=True)
    exponent = jnp.exp(scores - row_maxima)
    probabilities = exponent / jnp.sum(exponent, -1, keepdims=True)
    rounded = lax.optimization_barrier(probabilities.astype(jnp.bfloat16)).astype(jnp.float32)
    mixed_out = jnp.einsum("bshqk,bkshd->bqshd", rounded, value_rows)
    mixed_out = mixed_out.reshape(batch_count, frame_count, space_count, head_width).astype(
        jnp.bfloat16
    )
    grad_rows = grad_heads.reshape(
        batch_count, frame_count, space_count, head_count, head_size
    ).astype(jnp.float32)
    grad_probs = jnp.einsum("bqshd,bkshd->bshqk", grad_rows, value_rows)
    grad_values = jnp.einsum("bshqk,bqshd->bkshd", rounded, grad_rows)
    grad_scores = probabilities * (
        grad_probs - jnp.sum(grad_probs * probabilities, -1, keepdims=True)
    )
    grad_queries = jnp.einsum("bshqk,bkshd->bqshd", grad_scores, key_rows) * score_scale
    grad_keys = jnp.einsum("bshqk,bqshd->bkshd", grad_scores, queries) * score_scale
    grad_merged = jnp.stack([grad_queries, grad_keys, grad_values], 3)
    grad_merged = grad_merged.reshape(batch_count, frame_count, space_count, channel_count).astype(
        jnp.bfloat16
    )
    return (mixed_out, grad_merged)


def norm_backward(grad_norm, unit_rows, inverse, upstream_rows, row_onehot, gain):
    scaled = grad_norm * gain
    grad_hidden = upstream_rows.astype(jnp.float32) + inverse * (
        scaled - unit_rows * jnp.mean(scaled * unit_rows, -1, keepdims=True)
    )
    gain_term = jnp.sum(grad_norm * unit_rows, 0)
    action_term = jnp.einsum("ra,rd->ad", row_onehot, grad_hidden, precision=lax.Precision.HIGHEST)
    return (grad_hidden, gain_term, action_term)


def on_device(inputs, upstream, action_ids, frame_time, action_table, gain, w_qkv, w_out):
    batch_count, frame_count, space_count, feature_count = inputs.shape
    row_count = batch_count * frame_count * space_count
    channel_count = w_out.shape[1]
    onehot, inverse, unit_rows, normed = normalize(inputs, action_ids, action_table, gain)
    flat_norm = normed.reshape(row_count, feature_count)
    flat_up = upstream.reshape(row_count, feature_count)
    full_qkv = lax.all_gather(w_qkv, ("frame", "space"), axis=0, tiled=True)
    weight_flat = full_qkv.reshape(feature_count, 3 * channel_count)
    merged_qkv = jnp.dot(flat_norm, weight_flat, preferred_element_type=jnp.float32).astype(
        jnp.bfloat16
    )
    merged_qkv = merged_qkv.reshape(batch_count, frame_count, space_count, 3 * channel_count)
    grad_heads = jnp.dot(
        flat_up,
        lax.all_gather(w_out, ("frame", "space"), axis=0, tiled=True),
        preferred_element_type=jnp.float32,
    )
    grad_heads = grad_heads.astype(jnp.bfloat16).reshape(
        batch_count, frame_count, space_count, channel_count
    )
    timed_qkv, timed_grad = (
        lax.all_to_all(merged_qkv, "frame", split_axis=2, concat_axis=1, tiled=True),
        lax.all_to_all(grad_heads, "frame", split_axis=2, concat_axis=1, tiled=True),
    )
    mixed_out, grad_merged = temporal_attention(timed_qkv, timed_grad, frame_time, HEAD)
    back_mixed, back_grads = (
        lax.all_to_all(mixed_out, "frame", split_axis=1, concat_axis=2, tiled=True),
        lax.all_to_all(grad_merged, "frame", split_axis=1, concat_axis=2, tiled=True),
    )
    flat_mixed = back_mixed.reshape(row_count, channel_count)
    flat_grads = back_grads.reshape(row_count, 3 * channel_count)
    term_out = jnp.einsum("rd,re->de", flat_up, flat_mixed, preferred_element_type=jnp.float32)
    term_qkv = jnp.einsum(
        "rd,re->de", flat_norm, flat_grads, preferred_element_type=jnp.float32
    ).reshape(feature_count, 3, channel_count)
    grad_qkv, grad_out_proj = (
        lax.psum_scatter(term_qkv, ("frame", "space"), scatter_dimension=0, tiled=True),
        lax.psum_scatter(term_out, ("frame", "space"), scatter_dimension=0, tiled=True),
    )
    partial_norm = jnp.einsum(
        "rc,dc->rd", flat_grads, weight_flat, preferred_element_type=jnp.float32
    )
    action_count = onehot.shape[2]
    row_onehot = jnp.broadcast_to(
        onehot[:, :, None, :], (batch_count, frame_count, space_count, action_count)
    ).reshape(row_count, action_count)
    flat_unit = unit_rows.reshape(row_count, feature_count)
    flat_inverse = inverse.reshape(row_count, 1)
    grad_norm = lax.psum(partial_norm, "tensor")
    grad_hidden, gain_term, action_term = norm_backward(
        grad_norm, flat_unit, flat_inverse, flat_up, row_onehot, gain
    )
    grad_flat = grad_hidden.astype(jnp.bfloat16)
    grad_gain, grad_actions = lax.psum((gain_term, action_term), ("frame", "space"))
    grad_inputs = grad_flat.reshape(batch_count, frame_count, space_count, feature_count)
    return (grad_inputs, grad_qkv, grad_out_proj, grad_gain, grad_actions)


def solution(mesh):
    return jax.shard_map(
        on_device,
        mesh=mesh,
        in_specs=(
            P(None, "frame", "space", None),
            P(None, "frame", "space", None),
            P(None, "frame"),
            P(),
            P(),
            P(),
            P(("frame", "space"), None, "tensor"),
            P(("frame", "space"), "tensor"),
        ),
        out_specs=(
            P(None, "frame", "space", None),
            P(("frame", "space"), None, "tensor"),
            P(("frame", "space"), "tensor"),
            P(),
            P(),
        ),
        check_vma=False,
    )
```

profile of v0, /device:TPU:1, one launch (start us, length us, event | category | flops | bytes accessed | tf_op | source)
XLA Modules:
  0.0 807.6 jit_solution(10804012813414271570)
XLA Ops:
  9.6 2.4 multiply_reduce_fusion.2
  12.0 5.5 fusion.1
  17.5 60.2 %all-gather.5.cloned.1.call-done = bf16[2048,256]{1,0:T(8,128)(2,1)} async-done(((bf16[64,256]{1,0:T(8,128)(2,1)}), bf16[2048,256]{1,0:T(8,128)(2,1)}) %all-gather.5.cloned.1.call-update) | async-done | bytes 1048592 | tf_op jit(solution)/shard_map/all_gather | solution.py:91
  77.7 2.0 convolution_convert_fusion.3
  80.7 5.1 all-to-all-start.1
  85.8 60.6 %all-gather.3.cloned.1.call-done = bf16[2048,3,256]{2,0,1:T(8,128)(2,1)} async-done(((bf16[64,3,256]{2,0,1:T(8,128)(2,1)}), bf16[2048,3,256]{2,0,1:T(8,128)(2,1)}) %all-gather.3.cloned.1.call-update) | async-done | bytes 3145744 | tf_op jit(solution)/shard_map/all_gather | solution.py:83
  146.4 4.7 copy.58
  151.2 4.6 convolution_convert_fusion
  155.8 1.6 copy.59
  158.2 5.3 all-to-all-start
  163.8 1.9 copy.66
  165.7 1.9 reshape.106
  167.6 21.6 %all-to-all-done = bf16[2,2,144,768]{3,1,0,2:T(2,128)(2,1)S(1)} async-done(((bf16[2,2,144,768]{3,1,0,2:T(2,128)(2,1)}), bf16[2,2,144,768]{3,1,0,2:T(2,128)(2,1)S(1)}, u32[]{:S(2)}, u32[]{:S(2)}) %all-to-all-start) | async-done | bytes 884768 | tf_op jit(solution)/shard_map/all_to_all | solution.py:98
  189.2 1.5 copy.61
  190.7 3.1 reshape.104
  195.3 2.4 fusion.21
  197.7 1.7 multiply_reduce_fusion.3
  203.4 28.4 %all_to_all.60 = bf16[2,16,18,768]{3,0,2,1:T(2,128)(2,1)S(1)} all-to-all(bf16[2,16,18,768]{3,0,2,1:T(2,128)(2,1)} %reshape.114), channel_id=1, replica_groups=mesh['frame'=8,'space'=4,'tensor'=8] {'frame'}, dimensions={1} | all-to-all | bytes 1769472 | tf_op jit(solution)/shard_map/all_to_all | solution.py:104
  234.4 6.5 fusion.22
  242.6 13.3 %all_to_all.61 = bf16[2,16,18,256]{3,0,2,1:T(2,128)(2,1)S(1)} all-to-all(bf16[2,16,18,256]{3,0,2,1:T(2,128)(2,1)S(1)} %reshape.115), channel_id=1, replica_groups=mesh['frame'=8,'space'=4,'tensor'=8] {'frame'}, dimensions={1} | all-to-all | bytes 589824 | tf_op jit(solution)/shard_map/all_to_all | solution.py:103
  256.1 2.3 convolution_bitcast_fusion
  258.4 3.0 copy.88
  261.9 2.3 copy.74
  264.2 96.1 %all-reduce.3.cloned.1.call-done = f32[576,2048]{1,0:T(8,128)} async-done(((f32[576,2048]{1,0:T(8,128)}), f32[576,2048]{1,0:T(8,128)}) %all-reduce.3.cloned.1.call-update) | async-done | bytes 4718608 | tf_op jit(solution)/shard_map/psum | solution.py:125
  360.3 6.2 multiply_reduce_fusion
  368.0 2.7 fusion.19
  370.7 3.0 fusion.24
  373.8 5.4 fusion.23
  379.2 54.9 %psum.22 = f32[2048]{0:T(1024)} all-reduce(f32[2048]{0:T(1024)S(1)} %get-tuple-element.25), channel_id=1, replica_groups=mesh['frame'=8,'space'=4,'tensor'=8] {'frame','space'}, use_global_device_ids=true, to_apply=%region_9.10 | all-reduce | flops 2048 | bytes 16384 | tf_op jit(solution)/shard_map/psum | solution.py:130
  434.1 42.2 %reduce-scatter.7.cloned.1.call-done = f32[64,256]{1,0:T(8,128)} async-done(((f32[2048,256]{1,0:T(8,128)}), f32[64,256]{1,0:T(8,128)}) %reduce-scatter.7.cloned.1.call-update) | async-done | bytes 65552
  476.2 197.3 %all-reduce.5.cloned.1.call-done = f32[8,2048]{1,0:T(8,128)} async-done(((f32[8,2048]{1,0:T(8,128)}), f32[8,2048]{1,0:T(8,128)}) %all-reduce.5.cloned.1.call-update) | async-done | bytes 65552 | tf_op jit(solution)/shard_map/psum | solution.py:130
  673.5 125.8 %reduce-scatter.5.cloned.1.call-done = f32[64,3,256]{2,0,1:T(8,128)} async-done(((f32[2048,3,256]{2,0,1:T(8,128)}), f32[64,3,256]{2,0,1:T(8,128)}) %reduce-scatter.5.cloned.1.call-update) | async-done | bytes 196624 | tf_op jit(solution)/shard_map/reduce_scatter | solution.py:113
  (75 shorter events, 17.9 us)
Async XLA Ops:
  7.2 1.5 copy-start
  7.2 70.5 %all-gather.5.cloned.1.call-start = ((), (), s32[]{:S(2)}) async-start(), calls=%async_computation.7 | async-start | bytes 1081344 | tf_op jit(solution)/shard_map/all_gather | solution.py:91
  7.9 138.5 %all-gather.3.cloned.1.call-start = ((), (), s32[]{:S(2)}) async-start(), calls=%async_computation.6 | async-start | bytes 3244032 | tf_op jit(solution)/shard_map/all_gather | solution.py:83
  12.0 65.7 %copy-start.2 = (bf16[2,2,144,2048]{3,2,1,0:T(8,128)(2,1)S(1)}, bf16[2,2,144,2048]{3,2,1,0:T(8,128)(2,1)}, u32[]{:S(2)}) copy-start(bf16[2,2,144,2048]{3,2,1,0:T(8,128)(2,1)} %param.9) | copy-start | bytes 7077892
  80.7 76.8 %all-to-all-start.1 = ((bf16[2,2,144,256]{3,1,0,2:T(2,128)(2,1)}), bf16[2,2,144,256]{3,1,0,2:T(2,128)(2,1)S(1)}, u32[]{:S(2)}, u32[]{:S(2)}) async-start(bf16[2,2,144,256]{3,1,0,2:T(2,128)(2,1)} %copy.64), calls=%async_computation.1 | async-start | bytes 589824 | tf_op jit(solution)/shard_map/all_to_all | solution.py:99
  151.2 12.5 %copy-start.15 = (s32[2,16]{1,0:T(2,128)S(1)}, s32[2,16]{1,0:T(2,128)}, u32[]{:S(2)}) copy-start(s32[2,16]{1,0:T(2,128)} %param.11) | copy-start | bytes 388
  157.4 0.7 copy-start.9
  158.2 31.0 %all-to-all-start = ((bf16[2,2,144,768]{3,1,0,2:T(2,128)(2,1)}), bf16[2,2,144,768]{3,1,0,2:T(2,128)(2,1)S(1)}, u32[]{:S(2)}, u32[]{:S(2)}) async-start(bf16[2,2,144,768]{3,1,0,2:T(2,128)(2,1)} %copy.59), calls=%async_computation | async-start | bytes 1769472 | tf_op jit(solution)/shard_map/all_to_all | solution.py:98
  163.5 196.8 %all-reduce.3.cloned.1.call-start = ((), (), s32[]{:S(2)}) async-start(), calls=%async_computation.8 | async-start | bytes 9437184 | tf_op jit(solution)/shard_map/psum | solution.py:125
  195.3 4.1 copy-start.12
  195.3 5.6 copy-start.11
  197.7 3.2 copy-start.16
  197.7 3.4 copy-start.8
  199.3 1.8 copy-start.6
  234.4 6.5 copy-start.3
  240.9 1.0 copy-start.5
  240.9 1.0 copy-start.7
  240.9 235.3 %reduce-scatter.7.cloned.1.call-start = ((), (), s32[]{:S(2)}) async-start(), calls=%async_computation.11 | async-start | bytes 2162688
  256.1 5.7 copy-start.14
  258.4 101.8 %copy-start.13 = (f32[2048]{0:T(1024)S(1)}, f32[2048]{0:T(1024)}, u32[]{:S(2)}) copy-start(f32[2048]{0:T(1024)} %param.13) | copy-start | bytes 24580
  261.4 412.0 %all-reduce.5.cloned.1.call-start = ((), (), s32[]{:S(2)}) async-start(), calls=%async_computation.10 | async-start | bytes 131072 | tf_op jit(solution)/shard_map/psum | solution.py:130
  261.9 104.6 %slice-start = ((s8[4718592]{0:T(1024)(128)(4,1)}), s8[524288]{0:T(1024)(128)(4,1)S(1)}, s32[]{:S(2)}) async-start(s8[4718592]{0:T(1024)(128)(4,1)} %bitcast.92), calls=%async_computation.12 | async-start | bytes 1048576
  360.3 6.3 slice-start.1
  360.3 7.7 copy-start.1
  370.7 3.1 copy-start.4
  370.7 3.1 copy-start.10
  373.7 425.5 %reduce-scatter.5.cloned.1.call-start = ((), (), s32[]{:S(2)}) async-start(), calls=%async_computation.9 | async-start | bytes 6488064 | tf_op jit(solution)/shard_map/reduce_scatter | solution.py:113
Sparse Core Ops, SparseCore 0:
  9.9 67.7 all-gather.4
  79.6 66.7 all-gather.2
  241.0 119.2 all-reduce.2
  363.2 112.9 reduce-scatter.6
  479.5 193.9 all-reduce.4
  676.5 122.7 reduce-scatter.4
where the time goes:
time: 811 us; the launch traced here: 808 us
  waiting for transfers between devices  605 us (75%)
  blocking collectives  96.5 us (12%)
  local copies, waits for them, and re-layouts  32.4 us (4%)
  matrix products  31 us (4%)
  other arithmetic  17 us (2%)
  between operations  14.4 us (2%)
  starting transfers between devices  11.1 us (1%)
    psum x1, waiting for transfers between devices, on_device(): lax.psum((gain_term, action_term), ('frame', 'space'))  197 us
    reduce_scatter x1, waiting for transfers between devices, on_device(): lax.psum_scatter(term_qkv, ('frame', 'space'), scatter_dimension=0, tiled...  126 us
    psum x1, waiting for transfers between devices, on_device(): grad_norm = lax.psum(partial_norm, 'tensor')  96.1 us
    all_gather x1, waiting for transfers between devices, on_device(): full_qkv = lax.all_gather(w_qkv, ('frame', 'space'), axis=0, tiled=True)  60.6 us
    all_gather x1, waiting for transfers between devices, on_device(): lax.all_gather(w_out, ('frame', 'space'), axis=0, tiled=True)  60.2 us
    psum x1, blocking collectives, on_device(): lax.psum((gain_term, action_term), ('frame', 'space'))  54.9 us
    unnamed x7, waiting for transfers between devices  43.6 us
    all_to_all x1, blocking collectives, on_device(): lax.all_to_all(grad_merged, 'frame', split_axis=1, concat_axis=2, tiled=T...  28.4 us
  transfers between devices with their start and end apart: 8, of which 7 were waited for; matrix products, arithmetic and copies ran while one was open for 6% of the time, Pallas kernels for 0%

commit v1 on v0

v1 whole, which is shorter than its diff:
```python
import math

import jax
import jax.numpy as jnp
from jax import lax
from jax.experimental import pallas as pl
from jax.experimental.pallas import tpu as pltpu
from jax.sharding import PartitionSpec as P

HEAD = 128
NORM_EPSILON = 1e-06
MESH = pl.DeviceIdType.MESH
BF16 = jnp.bfloat16
F32 = jnp.float32

NZ, NX = 8, 4
SITES = 36
ROWS = 72
TOKENS = NZ * ROWS
SLICE = 256
VMEM_BYTES = 56 * 1024 * 1024


def position():
    f = lax.axis_index("frame")
    s = lax.axis_index("space")
    t = lax.axis_index("tensor")
    return f, s // 2, s % 2, t // NX, t % NX


def barrier(peers):
    sem = pltpu.get_barrier_semaphore()
    for peer in peers:
        pl.semaphore_signal(sem, inc=1, device_id=peer, device_id_type=MESH)
    pl.semaphore_wait(sem, len(peers))


class Copies:
    def __init__(self, send_sems, recv_sems):
        self.send_sems, self.recv_sems = send_sems, recv_sems
        self.started = []

    def send(self, slot, src, dst, device):
        copy = pltpu.make_async_remote_copy(
            src_ref=src,
            dst_ref=dst,
            send_sem=self.send_sems.at[slot],
            recv_sem=self.recv_sems.at[slot],
            device_id=device,
            device_id_type=MESH,
        )
        copy.start()
        self.started.append(copy)

    def arrived(self, slot, dst, device):
        pltpu.make_async_remote_copy(
            src_ref=dst,
            dst_ref=dst,
            send_sem=self.send_sems.at[slot],
            recv_sem=self.recv_sems.at[slot],
            device_id=device,
            device_id_type=MESH,
        ).wait_recv()

    def drain(self):
        for copy in self.started:
            copy.wait_send()


def mod(value, n):
    return lax.rem(value + 2 * n, n)


GATHER_SLOTS = 6 * NZ + 18


def gather_kernel(xu, w, tok, wts, send_sems, recv_sems, local_sems):
    f, yl, c, yh, x = position()
    right = {"tensor": yh * NX + mod(x + 1, NX)}
    left = {"tensor": yh * NX + mod(x - 1, NX)}
    other = {"tensor": (1 - yh) * NX + x}
    up, down = {"frame": mod(f + 1, NZ)}, {"frame": mod(f - 1, NZ)}
    ypeer = {"space": (1 - yl) * 2 + c}
    cpeer = {"space": yl * 2 + 1 - c}
    barrier([{"frame": mod(f + k, NZ)} for k in range(1, NZ)] + [right, left, other, ypeer, cpeer])

    cp = Copies(send_sems, recv_sems)
    xl, xr, xo = mod(x - 1, NX), mod(x + 1, NX), mod(x + 2, NX)
    W0 = 6 * NZ
    own_w = pltpu.make_async_copy(w, wts.at[f, yl, c], local_sems.at[1])
    own_w.start()
    cp.send(W0, w, wts.at[f, yl, c], ypeer)
    own = pltpu.make_async_copy(xu.at[f], tok.at[yh, x, f], local_sems.at[0])
    own.start()
    for k in range(1, NZ):
        j = mod(f + k, NZ)
        cp.send(6 * k, xu.at[j], tok.at[yh, x, f], {"frame": j})

    def stage_y(k):
        j = mod(f - k, NZ)
        if k == 0:
            own.wait()
        else:
            cp.arrived(6 * k, tok.at[yh, x, j], other)
        cp.send(6 * k + 1, tok.at[yh, x, j], tok.at[yh, x, j], other)

    def stage_x(k):
        j = mod(f - k, NZ)
        cp.arrived(6 * k + 1, tok.at[1 - yh, x, j], other)
        cp.send(6 * k + 2, tok.at[:, x, j], tok.at[:, x, j], right)
        cp.send(6 * k + 3, tok.at[:, x, j], tok.at[:, x, j], left)

    def stage_forward(k):
        j = mod(f - k, NZ)
        cp.arrived(6 * k + 2, tok.at[:, xl, j], left)
        cp.send(6 * k + 4, tok.at[:, xl, j, 0], tok.at[:, xl, j, 0], right)
        cp.arrived(6 * k + 3, tok.at[:, xr, j], right)
        cp.send(6 * k + 5, tok.at[:, xr, j, 1], tok.at[:, xr, j, 1], left)

    def ring(step):
        if step == 0:
            own_w.wait()
            cp.arrived(W0, wts.at[f, 1 - yl, c], ypeer)
            cp.send(W0 + 1, wts.at[f, :, c], wts.at[f, :, c], up)
            cp.send(W0 + 2, wts.at[f, :, c], wts.at[f, :, c], down)
            cp.send(W0 + 9, wts.at[f, :, c], wts.at[f, :, c], cpeer)
            return
        lo, hi = mod(f - step, NZ), mod(f + step, NZ)
        if step < 4:
            cp.arrived(W0 + 2 * step - 1, wts.at[lo, :, c], down)
            cp.arrived(W0 + 2 * step, wts.at[hi, :, c], up)
            if step < 3:
                cp.send(W0 + 2 * step + 1, wts.at[lo, :, c], wts.at[lo, :, c], up)
                cp.send(W0 + 2 * step + 2, wts.at[hi, :, c], wts.at[hi, :, c], down)
            else:
                cp.send(W0 + 7, wts.at[lo, 0, c], wts.at[lo, 0, c], up)
                cp.send(W0 + 8, wts.at[hi, 1, c], wts.at[hi, 1, c], down)
            cp.send(W0 + 9 + step, wts.at[lo, :, c], wts.at[lo, :, c], cpeer)
            cp.send(W0 + 12 + step, wts.at[hi, :, c], wts.at[hi, :, c], cpeer)
        else:
            cp.arrived(W0 + 7, wts.at[lo, 0, c], down)
            cp.arrived(W0 + 8, wts.at[lo, 1, c], up)
            cp.send(W0 + 16, wts.at[lo, :, c], wts.at[lo, :, c], cpeer)

    for k in range(NZ + 2):
        if k < NZ:
            stage_y(k)
        if 1 <= k <= NZ:
            stage_x(k - 1)
        if k >= 2:
            stage_forward(k - 2)
        if k in (0, 2, 4, 6, 8):
            ring(k // 2)
    for k in range(NZ):
        j = mod(f - k, NZ)
        cp.arrived(6 * k + 4, tok.at[:, xo, j, 0], left)
        cp.arrived(6 * k + 5, tok.at[:, xo, j, 1], right)
    for step in range(5):
        lo, hi = mod(f - step, NZ), mod(f + step, NZ)
        if step == 0:
            cp.arrived(W0 + 9, wts.at[f, :, 1 - c], cpeer)
        elif step < 4:
            cp.arrived(W0 + 9 + step, wts.at[lo, :, 1 - c], cpeer)
            cp.arrived(W0 + 12 + step, wts.at[hi, :, 1 - c], cpeer)
        else:
            cp.arrived(W0 + 16, wts.at[lo, :, 1 - c], cpeer)
    cp.drain()


def gather(xu, w):
    any_spec = pl.BlockSpec(memory_space=pl.ANY)
    return pl.pallas_call(
        gather_kernel,
        out_shape=(
            jax.ShapeDtypeStruct((2, NX, NZ, 2, ROWS, SLICE), BF16),
            jax.ShapeDtypeStruct((NZ, 2, 2, 64, 1024), BF16),
        ),
        in_specs=[any_spec, any_spec],
        out_specs=(any_spec, any_spec),
        scratch_shapes=[
            pltpu.SemaphoreType.DMA((GATHER_SLOTS,)),
            pltpu.SemaphoreType.DMA((GATHER_SLOTS,)),
            pltpu.SemaphoreType.DMA((2,)),
        ],
        compiler_params=pltpu.CompilerParams(
            collective_id=0, has_side_effects=True, vmem_limit_bytes=VMEM_BYTES
        ),
    )(xu, w)


def nt(a, b):
    return lax.dot_general(a, b, (((1,), (1,)), ((), ())), preferred_element_type=F32)


def tn(a, b):
    return lax.dot_general(a, b, (((0,), (0,)), ((), ())), preferred_element_type=F32)


def local_kernel(tok, wts, bias, gn, gw, normed, up, qkv, mixed, grads, probs, dscore):
    scale = 1.0 / math.sqrt(HEAD)
    for t in range(8):
        cols = slice(t * SLICE, (t + 1) * SLICE)
        for arr, out in ((0, normed), (1, up)):
            out[:, cols] = jnp.concatenate(
                [tok[t // NX, t % NX, j, arr].astype(F32) for j in range(NZ)], 0
            ).astype(BF16)

    @pl.loop(0, 4)
    def _(n):
        at = pl.ds(pl.multiple_of(n * 256, 256), 256)

        @pl.when(n < 3)
        def _():
            qkv[:, at] = jnp.dot(
                normed[...], wts[:, at], preferred_element_type=F32
            ).astype(BF16)

        @pl.when(n == 3)
        def _():
            qkv[:, at] = jnp.dot(up[...], wts[:, at], preferred_element_type=F32).astype(BF16)

    half = TOKENS // 2
    for h in range(2):
        q, k, v, g = (qkv[:, n * 256 + h * HEAD : n * 256 + (h + 1) * HEAD] for n in range(4))
        for part in range(2):
            rows = slice(part * half, (part + 1) * half)
            scores = nt(q[rows], k) * scale + bias[rows]
            exponent = jnp.exp(scores - jnp.max(scores, -1, keepdims=True))
            p = exponent / jnp.sum(exponent, -1, keepdims=True)
            probs[rows] = p.astype(BF16)
            gp = nt(g[rows], v)
            ds = p * (gp - jnp.sum(gp * p, -1, keepdims=True))
            dscore[rows] = ds.astype(BF16)
        lanes = slice(h * HEAD, (h + 1) * HEAD)
        pb, db = probs[...], dscore[...]
        mixed[:, lanes] = jnp.dot(pb, v, preferred_element_type=F32).astype(BF16)
        grads[:, h * HEAD : (h + 1) * HEAD] = (
            jnp.dot(db, k, preferred_element_type=F32) * scale
        ).astype(BF16)
        grads[:, 256 + h * HEAD : 256 + (h + 1) * HEAD] = (tn(db, q) * scale).astype(BF16)
        grads[:, 512 + h * HEAD : 512 + (h + 1) * HEAD] = tn(pb, g).astype(BF16)

    @pl.loop(0, 8)
    def _(t):
        at = pl.ds(pl.multiple_of(t * SLICE, SLICE), SLICE)
        back = nt(grads[...], wts[at, 0:768])
        for j in range(NZ):
            gn[t // NX, t % NX, j] = back[j * ROWS : (j + 1) * ROWS].astype(BF16)
        term = tn(normed[:, at], grads[...]).astype(BF16)
        term_out = tn(up[:, at], mixed[...]).astype(BF16)
        for r in range(4):
            gw[t, r // 2, r % 2, :, 0:768] = term[64 * r : 64 * r + 64]
            gw[t, r // 2, r % 2, :, 768:1024] = term_out[64 * r : 64 * r + 64]


def local(tok, wts, bias):
    spec = pl.BlockSpec(memory_space=pltpu.VMEM)
    return pl.pallas_call(
        local_kernel,
        out_shape=(
            jax.ShapeDtypeStruct((2, NX, NZ, ROWS, SLICE), BF16),
            jax.ShapeDtypeStruct((NZ, 2, 2, 64, 1024), BF16),
        ),
        in_specs=[spec] * 3,
        out_specs=(spec, spec),
        scratch_shapes=[
            pltpu.VMEM((TOKENS, 2048), BF16),
            pltpu.VMEM((TOKENS, 2048), BF16),
            pltpu.VMEM((TOKENS, 1024), BF16),
            pltpu.VMEM((TOKENS, 256), BF16),
            pltpu.VMEM((TOKENS, 768), BF16),
            pltpu.VMEM((TOKENS, TOKENS), BF16),
            pltpu.VMEM((TOKENS, TOKENS), BF16),
        ],
        compiler_params=pltpu.CompilerParams(vmem_limit_bytes=VMEM_BYTES),
    )(tok, wts.reshape(2048, 1024), bias)


BACK_SLOTS = 10 * NZ + 12


def back_kernel(
    gn, gw, full, wsum, part_l, part_r, sum_l, sum_r, in_l, in_r, ysend, yin, zsend,
    cin, rs_up, rs_down, ri_up, ri_down, psend, pin, send_sems, recv_sems, local_sems,
):
    f, yl, c, yh, x = position()
    right = {"tensor": yh * NX + mod(x + 1, NX)}
    left = {"tensor": yh * NX + mod(x - 1, NX)}
    other = {"tensor": (1 - yh) * NX + x}
    up, down = {"frame": mod(f + 1, NZ)}, {"frame": mod(f - 1, NZ)}
    ypeer = {"space": (1 - yl) * 2 + c}
    cpeer = {"space": yl * 2 + 1 - c}
    barrier([{"frame": mod(f + k, NZ)} for k in range(1, NZ)] + [right, left, other, ypeer, cpeer])

    cp = Copies(send_sems, recv_sems)
    xl, xr, xo = mod(x - 1, NX), mod(x + 1, NX), mod(x + 2, NX)
    lo_lanes, hi_lanes = pl.ds(0, 128), pl.ds(128, 128)
    W0 = 10 * NZ

    for k in range(NZ):
        j = mod(f + k, NZ)
        cp.send(10 * k, gn.at[:, xo, j, :, lo_lanes], part_l.at[k], right)
        cp.send(10 * k + 1, gn.at[:, xo, j, :, hi_lanes], part_r.at[k], left)
        if k == 0:
            cp.send(W0, gw.at[:, :, 1 - c], cin, cpeer)

    def stage_sum(k):
        j = mod(f + k, NZ)
        cp.arrived(10 * k, part_l.at[k], left)
        sum_r[k, :, :, 0:128] = (
            gn[:, xr, j, :, 0:128].astype(F32) + part_l[k].astype(F32)
        ).astype(BF16)
        sum_r[k, :, :, 128:256] = gn[:, xr, j, :, 128:256]
        cp.send(10 * k + 2, sum_r.at[k], in_l.at[k], right)
        cp.arrived(10 * k + 1, part_r.at[k], right)
        sum_l[k, :, :, 0:128] = gn[:, xl, j, :, 0:128]
        sum_l[k, :, :, 128:256] = (
            gn[:, xl, j, :, 128:256].astype(F32) + part_r[k].astype(F32)
        ).astype(BF16)
        cp.send(10 * k + 3, sum_l.at[k], in_r.at[k], left)

    def stage_y(k):
        j = mod(f + k, NZ)
        cp.arrived(10 * k + 2, in_l.at[k], left)
        cp.arrived(10 * k + 3, in_r.at[k], right)
        theirs = (
            gn[1 - yh, x, j].astype(F32)
            + in_l[k, 1 - yh].astype(F32)
            + in_r[k, 1 - yh].astype(F32)
        )
        ysend[k] = theirs.astype(BF16)
        cp.send(10 * k + 4, ysend.at[k], yin.at[k], other)

    def stage_z(k):
        j = mod(f + k, NZ)
        cp.arrived(10 * k + 4, yin.at[k], other)
        mine = (
            gn[yh, x, j].astype(F32)
            + in_l[k, yh].astype(F32)
            + in_r[k, yh].astype(F32)
            + yin[k].astype(F32)
        )
        zsend[k] = mine.astype(BF16)
        if k == 0:
            pltpu.make_async_copy(zsend.at[0], full.at[yh, x, f], local_sems.at[0]).start()
        else:
            cp.send(10 * k + 5, zsend.at[k], full.at[yh, x, f], {"frame": j})

    def gather_y(k):
        j = mod(f - k, NZ)
        if k == 0:
            pltpu.make_async_copy(zsend.at[0], full.at[yh, x, f], local_sems.at[0]).wait()
        else:
            cp.arrived(10 * k + 5, full.at[yh, x, j], other)
        cp.send(10 * k + 6, full.at[yh, x, j], full.at[yh, x, j], other)

    def gather_x(k):
        j = mod(f - k, NZ)
        cp.arrived(10 * k + 6, full.at[1 - yh, x, j], other)
        cp.send(10 * k + 7, full.at[:, x, j], full.at[:, x, j], right)
        cp.send(10 * k + 8, full.at[:, x, j], full.at[:, x, j], left)

    def gather_forward(k):
        j = mod(f - k, NZ)
        cp.arrived(10 * k + 7, full.at[:, xl, j], left)
        here = full.at[:, xl, j, :, lo_lanes]
        cp.send(10 * k + 9, here, here, right)
        cp.arrived(10 * k + 8, full.at[:, xr, j], right)
        here = full.at[:, xr, j, :, hi_lanes]
        cp.send(W0 + 12 + k, here, here, left)

    def block(j, row):
        return gw[j, row, c].astype(F32) + cin[j, row].astype(F32)

    def ring(step):
        if step == 0:
            cp.arrived(W0, cin, cpeer)
            far = mod(f + 4, NZ)
            rs_up[0, 0] = block(far, 0).astype(BF16)
            cp.send(W0 + 1, rs_up.at[0, 0], ri_up.at[0, 0], up)
            rs_down[0, 0] = block(far, 1).astype(BF16)
            cp.send(W0 + 2, rs_down.at[0, 0], ri_down.at[0, 0], down)
            return
        if step < 4:
            ahead, behind = mod(f + 4 - step, NZ), mod(f - 4 + step, NZ)
            if step == 1:
                cp.arrived(W0 + 1, ri_up.at[0, 0], down)
                rs_up[1, 0] = (block(ahead, 0) + ri_up[0, 0].astype(F32)).astype(BF16)
                rs_up[1, 1] = block(ahead, 1).astype(BF16)
                cp.send(W0 + 3, rs_up.at[1], ri_up.at[1], up)
                cp.arrived(W0 + 2, ri_down.at[0, 0], up)
                rs_down[1, 0] = block(behind, 0).astype(BF16)
                rs_down[1, 1] = (block(behind, 1) + ri_down[0, 0].astype(F32)).astype(BF16)
                cp.send(W0 + 4, rs_down.at[1], ri_down.at[1], down)
            else:
                cp.arrived(W0 + 2 * step - 1, ri_up.at[step - 1], down)
                for r in range(2):
                    rs_up[step, r] = (
                        block(ahead, r) + ri_up[step - 1, r].astype(F32)
                    ).astype(BF16)
                cp.send(W0 + 2 * step + 1, rs_up.at[step], ri_up.at[step], up)
                cp.arrived(W0 + 2 * step, ri_down.at[step - 1], up)
                for r in range(2):
                    rs_down[step, r] = (
                        block(behind, r) + ri_down[step - 1, r].astype(F32)
                    ).astype(BF16)
                cp.send(W0 + 2 * step + 2, rs_down.at[step], ri_down.at[step], down)
            return
        if step == 4:
            cp.arrived(W0 + 7, ri_up.at[3], down)
            cp.arrived(W0 + 8, ri_down.at[3], up)
            theirs = (
                block(f, 1 - yl)
                + ri_up[3, 1 - yl].astype(F32)
                + ri_down[3, 1 - yl].astype(F32)
            )
            psend[...] = theirs.astype(BF16)
            cp.send(W0 + 9, psend, pin, ypeer)
            return
        cp.arrived(W0 + 9, pin, ypeer)
        wsum[...] = (
            block(f, yl)
            + ri_up[3, yl].astype(F32)
            + ri_down[3, yl].astype(F32)
            + pin[...].astype(F32)
        )

    stages = [stage_sum, stage_y, stage_z, gather_y, gather_x, gather_forward]
    for k in range(NZ + len(stages) - 1):
        for lag, stage in enumerate(stages):
            if 0 <= k - lag < NZ:
                stage(k - lag)
        if k % 2 == 1 and k // 2 < 6:
            ring(k // 2)
    for k in range(NZ):
        j = mod(f - k, NZ)
        cp.arrived(10 * k + 9, full.at[:, xo, j, :, lo_lanes], left)
        cp.arrived(W0 + 12 + k, full.at[:, xo, j, :, hi_lanes], right)
    cp.drain()


def back(gn, gw):
    spec = pl.BlockSpec(memory_space=pltpu.VMEM)
    any_spec = pl.BlockSpec(memory_space=pl.ANY)
    slots = BACK_SLOTS + NZ
    block = (2, ROWS, SLICE)
    return pl.pallas_call(
        back_kernel,
        out_shape=(
            jax.ShapeDtypeStruct((2, NX, NZ, ROWS, SLICE), BF16),
            jax.ShapeDtypeStruct((64, 1024), F32),
        ),
        in_specs=[spec, spec],
        out_specs=(any_spec, spec),
        scratch_shapes=[
            pltpu.VMEM((NZ, 2, ROWS, 128), BF16),
            pltpu.VMEM((NZ, 2, ROWS, 128), BF16),
            pltpu.VMEM((NZ,) + block, BF16),
            pltpu.VMEM((NZ,) + block, BF16),
            pltpu.VMEM((NZ,) + block, BF16),
            pltpu.VMEM((NZ,) + block, BF16),
            pltpu.VMEM((NZ, ROWS, SLICE), BF16),
            pltpu.VMEM((NZ, ROWS, SLICE), BF16),
            pltpu.VMEM((NZ, ROWS, SLICE), BF16),
            pltpu.VMEM((NZ, 2, 64, 1024), BF16),
            pltpu.VMEM((4, 2, 64, 1024), BF16),
            pltpu.VMEM((4, 2, 64, 1024), BF16),
            pltpu.VMEM((4, 2, 64, 1024), BF16),
            pltpu.VMEM((4, 2, 64, 1024), BF16),
            pltpu.VMEM((64, 1024), BF16),
            pltpu.VMEM((64, 1024), BF16),
            pltpu.SemaphoreType.DMA((slots,)),
            pltpu.SemaphoreType.DMA((slots,)),
            pltpu.SemaphoreType.DMA((1,)),
        ],
        compiler_params=pltpu.CompilerParams(
            collective_id=1, has_side_effects=True, vmem_limit_bytes=VMEM_BYTES
        ),
    )(gn, gw)


def small_kernel(term, out, zin, sent, sin, total, send_sems, recv_sems):
    f, yl, c, yh, x = position()
    s, t = yl * 2 + c, yh * NX + x
    frames = [{"frame": mod(f + k, NZ)} for k in range(1, NZ)]
    spaces = [{"space": mod(s + k, 4)} for k in range(1, 4)]
    tensors = [{"tensor": mod(t + k, 8)} for k in range(1, 8)]
    barrier(frames + spaces + tensors)
    cp = Copies(send_sems, recv_sems)
    zin[f] = term[t]
    for k in range(1, NZ):
        cp.send(k - 1, term.at[t], zin.at[f], frames[k - 1])
    for k in range(1, NZ):
        cp.arrived(k - 1, zin.at[mod(f - k, NZ)], frames[k - 1])
    acc = zin[0]
    for k in range(1, NZ):
        acc = acc + zin[k]
    sent[...] = acc
    sin[s] = acc
    for k in range(1, 4):
        cp.send(6 + k, sent, sin.at[s], spaces[k - 1])
    for k in range(1, 4):
        cp.arrived(6 + k, sin.at[mod(s - k, 4)], spaces[k - 1])
    acc = sin[0]
    for k in range(1, 4):
        acc = acc + sin[k]
    total[...] = acc
    out[t] = acc
    for k in range(1, 8):
        cp.send(9 + k, total, out.at[t], tensors[k - 1])
    for k in range(1, 8):
        cp.arrived(9 + k, out.at[mod(t - k, 8)], tensors[k - 1])
    cp.drain()


def small_sum(term):
    spec = pl.BlockSpec(memory_space=pltpu.VMEM)
    return pl.pallas_call(
        small_kernel,
        out_shape=jax.ShapeDtypeStruct((8, 16, SLICE), F32),
        in_specs=[spec],
        out_specs=spec,
        scratch_shapes=[
            pltpu.VMEM((NZ, 16, SLICE), F32),
            pltpu.VMEM((16, SLICE), F32),
            pltpu.VMEM((4, 16, SLICE), F32),
            pltpu.VMEM((16, SLICE), F32),
            pltpu.SemaphoreType.DMA((17,)),
            pltpu.SemaphoreType.DMA((17,)),
        ],
        compiler_params=pltpu.CompilerParams(collective_id=2, has_side_effects=True),
    )(term)


def score_bias(frame_time):
    rollout = lax.axis_index("frame") // 4
    times = lax.dynamic_index_in_dim(frame_time, rollout, 0, keepdims=False)
    times = jnp.broadcast_to(times[:, None], (2 * NZ, SITES)).reshape(TOKENS)
    sites = jnp.broadcast_to(jnp.arange(SITES)[None, :], (2 * NZ, SITES)).reshape(TOKENS)
    allowed = (sites[:, None] == sites[None, :]) & (times[None, :] <= times[:, None])
    return jnp.where(allowed, 0.0, -1e30).astype(F32)


def by_site(rows):
    n = rows.shape[-1]
    return rows.reshape(2, 2, 4, SITES, n).transpose(0, 2, 1, 3, 4).reshape(NZ, ROWS, n)


def on_device(inputs, upstream, action_ids, frame_time, action_table, gain, w_qkv, w_out):
    t = lax.axis_index("tensor")
    actions = action_table.shape[0]
    onehot = (action_ids[..., None] == jnp.arange(actions, dtype=jnp.int32)).astype(F32)
    embedded = jnp.einsum("bfa,ad->bfd", onehot, action_table, precision=lax.Precision.HIGHEST)
    hidden = inputs.astype(F32) + embedded[:, :, None, :]
    inverse = lax.rsqrt(jnp.mean(hidden * hidden, -1, keepdims=True) + NORM_EPSILON)

    def mine(a):
        return lax.dynamic_slice_in_dim(a, t * SLICE, SLICE, axis=a.ndim - 1)

    normed = (mine(inputs).astype(F32) + mine(embedded)[:, :, None, :]) * inverse * mine(gain)
    xu = jnp.stack([by_site(normed.astype(BF16)), by_site(mine(upstream))], 1)
    w = jnp.concatenate([w_qkv.reshape(64, 768), w_out], 1)

    tok, wts = gather(xu, w)
    gn, gw = local(tok, wts, score_bias(frame_time))
    full, wsum = back(gn, gw)

    grad_norm = full.reshape(8, 2, 4, 2, SITES, SLICE).transpose(1, 3, 2, 4, 0, 5)
    grad_norm = grad_norm.reshape(inputs.shape).astype(F32)
    unit_rows = hidden * inverse
    scaled = grad_norm * gain
    grad_hidden = upstream.astype(F32) + inverse * (
        scaled - unit_rows * jnp.mean(scaled * unit_rows, -1, keepdims=True)
    )
    gain_term = jnp.sum(grad_norm * unit_rows, (0, 1, 2))
    frame_sums = jnp.sum(grad_hidden, 2)
    action_term = jnp.einsum("bfa,bfd->ad", onehot, frame_sums, precision=lax.Precision.HIGHEST)
    term = jnp.concatenate([jnp.broadcast_to(gain_term[None], (8, 2048)), action_term], 0)
    sums = small_sum(term.reshape(16, 8, SLICE).transpose(1, 0, 2))
    sums = sums.transpose(1, 0, 2).reshape(16, 2048)
    return (
        grad_hidden.astype(BF16),
        wsum[:, :768].reshape(64, 3, 256),
        wsum[:, 768:],
        sums[0],
        sums[8:],
    )


def solution(mesh):
    return jax.shard_map(
        on_device,
        mesh=mesh,
        in_specs=(
            P(None, "frame", "space", None),
            P(None, "frame", "space", None),
            P(None, "frame"),
            P(),
            P(),
            P(),
            P(("frame", "space"), None, "tensor"),
            P(("frame", "space"), "tensor"),
        ),
        out_specs=(
            P(None, "frame", "space", None),
            P(("frame", "space"), None, "tensor"),
            P(("frame", "space"), "tensor"),
            P(),
            P(),
        ),
        check_vma=False,
    )
```

time: 811 us -> 225 us (0.28)
  waiting for transfers between devices: 605 us -> 0 us
  Pallas kernels: 0 us -> 174 us
  blocking collectives: 96.5 us -> 0 us
  matrix products: 31 us -> 1.21 us
  between operations: 14.4 us -> 0.85 us
  starting transfers between devices: 11.1 us -> 0 us
    psum x2 -> x0, waiting for transfers between devices: 293 us -> none  [the longest x1 197 us: on_device(): lax.psum((gain_term, action_term), ('frame', 'space'))]
    pallas_call x0 -> x4, Pallas kernels: none -> 174 us  [the longest x1 63.2 us: gather(): pl.pallas_call(gather_kernel, out_shape=(jax.ShapeDtypeStruct((2, NX, NZ,...]
    reduce_scatter x1 -> x0, waiting for transfers between devices: 126 us -> none  [on_device(): lax.psum_scatter(term_qkv, ('frame', 'space'), scatter_dimension=0, tiled...]
    all_gather x2 -> x0, waiting for transfers between devices: 121 us -> none  [the longest x1 60.6 us: on_device(): full_qkv = lax.all_gather(w_qkv, ('frame', 'space'), axis=0, tiled=True)]
    psum x1 -> x0, blocking collectives: 54.9 us -> none  [on_device(): lax.psum((gain_term, action_term), ('frame', 'space'))]
    unnamed x7 -> x0, waiting for transfers between devices: 43.6 us -> none
    all_to_all x2 -> x0, blocking collectives: 41.7 us -> none  [the longest x1 28.4 us: on_device(): lax.all_to_all(grad_merged, 'frame', split_axis=1, concat_axis=2, tiled=T...]
    dot_general x12 -> x2, matrix products: 28.6 us -> 1.21 us  [the longest x1 0.91 us: on_device(): jnp.einsum('bfa,ad->bfd', onehot, action_table, precision=lax.Precision.H...]
  transfers between devices with their start and end apart: 8 -> 0, of which waited for: 7 -> 0; matrix products, arithmetic and copies ran while one was open for 6% -> 0% of each run, Pallas kernels for 0% -> 0%
where the time goes in v1:
time: 225 us; the launch traced here: 224 us
  Pallas kernels  174 us (77%)
  local copies, waits for them, and re-layouts  33.2 us (15%)
  other arithmetic  14.3 us (6%)
    pallas_call x1, Pallas kernels, gather(): pl.pallas_call(gather_kernel, out_shape=(jax.ShapeDtypeStruct((2, NX, NZ,...  63.2 us
    pallas_call x1, Pallas kernels, back(): pl.pallas_call(back_kernel, out_shape=(jax.ShapeDtypeStruct((2, NX, NZ, R...  59.4 us
    pallas_call x1, Pallas kernels, small_sum(): pl.pallas_call(small_kernel, out_shape=jax.ShapeDtypeStruct((8, 16, SLICE...  30.7 us
    convert_element_type x4, local copies, waits for them, and re-layouts, on_device(): grad_norm = grad_norm.reshape(inputs.shape).astype(F32)  21.3 us
    pallas_call x1, Pallas kernels, local(): pl.pallas_call(local_kernel, out_shape=(jax.ShapeDtypeStruct((2, NX, NZ,...  21 us

profile of v1, /device:TPU:1, one launch (start us, length us, event | category | flops | bytes accessed | tf_op | source)
XLA Modules:
  0.0 223.8 jit_solution(6805463906621858593)
XLA Ops:
  0.7 0.7 fusion.7
  1.4 0.8 dynamic_slice.18
  2.2 0.1 le.15
  2.4 0.9 fusion.3
  3.3 2.4 %multiply_reduce_fusion.2 = f32[2,2,144]{2,1,0:T(2,128)S(1)} fusion(bf16[2,2,144,2048]{3,2,1,0:T(8,128)(2,1)} %param.8, f32[2,2,2048]{2,1,0:T(2,128)S(1)} %fusion.3), kind=kLoop, calls=%fused_computation.4 | loop fusion | flops 4718016 | bytes 2394368 | tf_op jit(solution)/shard_map/reduce_sum | solution.py:555
  5.7 0.9 copy.45
  6.6 1.4 pad_maximum_fusion.1.w
  8.0 1.1 multiply_convert_fusion
  9.1 0.2 copy.27
  9.5 1.0 constant_dynamic-slice_fusion.1
  10.5 0.2 copy.29
  10.8 0.9 pad_maximum_fusion.xu
  11.7 1.4 and_select_fusion.bias
  13.1 63.2 %shard_map.119 = (bf16[2,4,8,2,72,256]{5,4,3,2,1,0:T(8,128)(2,1)}, bf16[8,2,2,64,1024]{4,3,2,1,0:T(8,128)(2,1)}) custom-call(bf16[8,2,72,256]{3,2,1,0:T(8,128)(2,1)} %pad_maximum_fusion.xu, bf16[64,1024]{1,0:T(8,128)(2,1)} %pad_maximum_fusion.1.w), custom_call_target="tpu_custom_call" | custom-call | tf_op jit(solution)/shard_map/pallas_call | solution.py:172
  76.2 21.0 %shard_map.120 = (bf16[2,4,8,72,256]{4,3,2,1,0:T(8,128)(2,1)}, bf16[8,2,2,64,1024]{4,3,2,1,0:T(8,128)(2,1)}) custom-call(bf16[2,4,8,2,72,256]{5,4,3,2,1,0:T(8,128)(2,1)} %get-tuple-element.11.tok, bf16[2048,1024]{1,0:T(8,128)(2,1)} %bitcast.39, f32[576,576]{1,0:T(8,128)} %and_select_fusion.bias), custom_call_target="tpu_custom_call" | custom-call | tf_op jit(solution)/shard_map/pallas_call | solution.py:258
  97.3 59.4 %shard_map.121 = (bf16[2,4,8,72,256]{4,3,2,1,0:T(8,128)(2,1)}, f32[64,1024]{1,0:T(8,128)}) custom-call(bf16[2,4,8,72,256]{4,3,2,1,0:T(8,128)(2,1)} %get-tuple-element.13.gn, bf16[8,2,2,64,1024]{4,3,2,1,0:T(8,128)(2,1)} %get-tuple-element.14.gw), custom_call_target="tpu_custom_call" | custom-call | tf_op jit(solution)/shard_map/pallas_call | solution.py:447
  156.7 1.5 slice.17
  158.2 0.9 slice.16
  159.1 0.7 copy.50
  159.8 4.8 %reshape.74 = f32[8,2,4,2,36,256]{5,4,3,2,1,0:T(8,128)} reshape(bf16[2,4,8,72,256]{4,3,2,1,0:T(8,128)(2,1)} %get-tuple-element.15) | data formatting | bytes 7077888 | tf_op jit(solution)/shard_map/convert_element_type | solution.py:569
  164.6 5.5 %copy.49 = f32[8,2,4,2,36,256]{5,2,1,4,3,0:T(4,128)S(1)} copy(f32[8,2,4,2,36,256]{5,4,3,2,1,0:T(8,128)} %reshape.74) | data formatting | bytes 9437184 | tf_op jit(solution)/shard_map/convert_element_type | solution.py:569
  170.1 4.9 %copy.35 = f32[2,2,4,36,8,256]{5,4,3,2,1,0:T(8,128)} copy(f32[2,2,4,36,8,256]{5,2,0,3,1,4:T(4,128)S(1)} %bitcast.38) | data formatting | bytes 9437184 | tf_op jit(solution)/shard_map/convert_element_type | solution.py:569
  175.0 6.2 %reshape.68 = f32[2,2,144,2048]{3,2,1,0:T(8,128)} reshape(f32[2,2,4,36,8,256]{5,4,3,2,1,0:T(8,128)} %copy.35) | data formatting | bytes 9437184 | tf_op jit(solution)/shard_map/convert_element_type | solution.py:569
  181.2 3.6 %multiply_reduce_fusion.1 = f32[2,2,144]{2,1,0:T(2,128)S(1)} fusion(bf16[2,2,144,2048]{3,2,1,0:T(8,128)(2,1)S(1)} %copy-done.2, f32[2,2,144,2048]{3,2,1,0:T(8,128)} %reshape.68, f32[2048]{0:T(1024)S(1)} %copy-done.4, f32[2,2,144]{2,1,0:T(2,128)S(1)} %add_rsqrt_fusion, f32[2,2,2048]{2,1,0:T(2,128)S(1)} %fusion.3), kind=kLoop, calls=%fused_computation.3 | loop fusion | flops 7077312 | bytes 7123456 | tf_op jit(solution)/shard_map/reduce_sum | solution.py:573
  184.8 0.2 copy-done.1
  184.9 0.8 copy-done.3
  185.7 3.5 %multiply_reduce_fusion = (f32[2048]{0:T(1024)S(1)}, f32[2,2,2048]{2,1,0:T(2,128)S(1)}, bf16[2,2,144,2048]{3,2,1,0:T(8,128)(2,1)}) fusion(f32[2,2,144,2048]{3,2,1,0:T(8,128)S(1)} %copy-done.1, bf16[2,2,144,2048]{3,2,1,0:T(8,128)(2,1)S(1)} %copy-done.2, f32[2,2,144]{2,1,0:T(2,128)S(1)} %add_rsqrt_fusion, f32[2,2,2048]{2,1,0:T(2,128)S(1)} %fusion.3, ...), kind=kLoop, calls=%fused_computation.1 | loop fusion | flops 15325184 | bytes 11883008 | tf_op jit(solution)/shard_map/reduce_sum | solution.py:575
  189.2 0.3 convolution_bitcast_fusion
  189.6 0.6 copy.51
  190.2 30.7 %shard_map.122 = f32[8,16,256]{2,1,0:T(8,128)} custom-call(f32[8,16,256]{2,1,0:T(8,128)} %bitcast.44), custom_call_target="tpu_custom_call" | custom-call | tf_op jit(solution)/shard_map/pallas_call | solution.py:518
  220.9 1.4 slice.21
  222.4 1.5 slice.22
  (22 shorter events, 0.4 us)
Async XLA Ops:
  0.6 1.7 copy-start
  175.0 6.2 %copy-start.2 = (bf16[2,2,144,2048]{3,2,1,0:T(8,128)(2,1)S(1)}, bf16[2,2,144,2048]{3,2,1,0:T(8,128)(2,1)}, u32[]{:S(2)}) copy-start(bf16[2,2,144,2048]{3,2,1,0:T(8,128)(2,1)} %param.8) | copy-start | bytes 7077892
  175.0 6.2 %copy-start.4 = (f32[2048]{0:T(1024)S(1)}, f32[2048]{0:T(1024)}, u32[]{:S(2)}) copy-start(f32[2048]{0:T(1024)} %param.13) | copy-start | bytes 24580
  181.2 3.8 %copy-start.1 = (f32[2,2,144,2048]{3,2,1,0:T(8,128)S(1)}, f32[2,2,144,2048]{3,2,1,0:T(8,128)}, u32[]{:S(2)}) copy-start(f32[2,2,144,2048]{3,2,1,0:T(8,128)} %reshape.68) | copy-start | bytes 14155780
  181.2 4.5 %copy-start.3 = (bf16[2,2,144,2048]{3,2,1,0:T(8,128)(2,1)S(1)}, bf16[2,2,144,2048]{3,2,1,0:T(8,128)(2,1)}, u32[]{:S(2)}) copy-start(bf16[2,2,144,2048]{3,2,1,0:T(8,128)(2,1)} %param.9) | copy-start | bytes 7077892
  185.7 3.5 %copy-start.5 = (s32[2,2]{1,0:T(2,128)S(1)}, s32[2,2]{1,0:T(2,128)}, u32[]{:S(2)}) copy-start(s32[2,2]{1,0:T(2,128)} %param.10) | copy-start | bytes 52

commit v2 on v0

v2 whole, which is shorter than its diff:
```python
import math

import jax
import jax.numpy as jnp
from jax import lax
from jax.experimental import pallas as pl
from jax.experimental.pallas import tpu as pltpu
from jax.sharding import PartitionSpec as P

HEAD = 128
NORM_EPSILON = 1e-06
MESH = pl.DeviceIdType.MESH
BF16 = jnp.bfloat16
F32 = jnp.float32

NZ, NX, NT = 8, 4, 8
SITES = 36
ROWS = 72
TOKENS = NZ * ROWS
SLICE = 256
WIDTH = 2048
VMEM_BYTES = 58 * 1024 * 1024
ORDER = (0, 1, 7, 2, 6, 3, 5, 4)
SLOTS = 320


def mod(value, n):
    return lax.rem(value + 2 * n, n)


def nt(a, b):
    return lax.dot_general(a, b, (((1,), (1,)), ((), ())), preferred_element_type=F32)


def tn(a, b):
    return lax.dot_general(a, b, (((0,), (0,)), ((), ())), preferred_element_type=F32)


def nn(a, b):
    return jnp.dot(a, b, preferred_element_type=F32)


class Copies:
    def __init__(self, send_sems, recv_sems):
        self.send_sems, self.recv_sems = send_sems, recv_sems
        self.slots, self.started = {}, []

    def slot(self, name):
        return self.slots.setdefault(name, len(self.slots))

    def send(self, name, src, dst, device):
        slot = self.slot(name)
        copy = pltpu.make_async_remote_copy(
            src_ref=src,
            dst_ref=dst,
            send_sem=self.send_sems.at[slot],
            recv_sem=self.recv_sems.at[slot],
            device_id=device,
            device_id_type=MESH,
        )
        copy.start()
        self.started.append(copy)

    def arrived(self, name, dst, device):
        slot = self.slot(name)
        pltpu.make_async_remote_copy(
            src_ref=dst,
            dst_ref=dst,
            send_sem=self.send_sems.at[slot],
            recv_sem=self.recv_sems.at[slot],
            device_id=device,
            device_id_type=MESH,
        ).wait_recv()

    def drain(self):
        for copy in self.started:
            copy.wait_send()


def kernel(
    inputs, upstream, w3, wo, embedded, ids, gain, code_col, code_row,
    out, wq_sum, wo_sum, small_out,
    in_v, up_v, xu, meta, meta_in, tok, wts, normed, up, bias, qkv, mixed, grads, probs, dscore,
    m_part, m_in, m_sum, gn, gw, part_l, part_r, sum_l, sum_r, in_l, in_r, ysend, yin, zsend,
    cin, rs_up, rs_down, ri_up, ri_down, psend, pin, full,
    act, gterm, small, zin, sent, sin, total,
    send_sems, recv_sems, local_sems,
):
    f = lax.axis_index("frame")
    s = lax.axis_index("space")
    t = lax.axis_index("tensor")
    yl, c, yh, x = s // 2, s % 2, t // NX, t % NX
    xl, xr, xo = mod(x - 1, NX), mod(x + 1, NX), mod(x + 2, NX)
    right, left = {"tensor": yh * NX + xr}, {"tensor": yh * NX + xl}
    other = {"tensor": (1 - yh) * NX + x}
    z_up, z_down = {"frame": mod(f + 1, NZ)}, {"frame": mod(f - 1, NZ)}
    ypeer = {"space": (1 - yl) * 2 + c}
    cpeer = {"space": yl * 2 + 1 - c}
    frames = [{"frame": mod(f + k, NZ)} for k in range(1, NZ)]
    spaces = [{"space": mod(s + k, 4)} for k in range(1, 4)]
    tensors = [{"tensor": mod(t + k, NT)} for k in range(1, NT)]
    peers = frames + spaces + tensors
    my_cols = pl.ds(pl.multiple_of(t * SLICE, SLICE), SLICE)

    greeted = pltpu.get_barrier_semaphore()
    for peer in peers:
        pl.semaphore_signal(greeted, inc=1, device_id=peer, device_id_type=MESH)

    cp = Copies(send_sems, recv_sems)

    def w_rows(z, row, plane):
        return wts.at[pl.ds(pl.multiple_of((z * 4 + row * 2 + plane) * 64, 64), 64), :]

    def local(src, dst, n):
        copy = pltpu.make_async_copy(src, dst, local_sems.at[n])
        copy.start()
        return copy

    load_in = local(inputs, in_v, 0)
    load_up = local(upstream.at[:, :, my_cols], up_v, 1)
    own_rows = pl.ds(pl.multiple_of((f * 4 + s) * 64, 64), 64)
    load_w = [
        local(w3.at[n], wts.at[own_rows, n * 256 : (n + 1) * 256], 2 + n) for n in range(3)
    ] + [local(wo, wts.at[own_rows, 768:1024], 5)]
    load_in.wait()

    lane = lax.broadcasted_iota(jnp.int32, (ROWS, 128), 1)
    eye = (lane == lax.broadcasted_iota(jnp.int32, (ROWS, 128), 0)).astype(F32)

    def to_row(column):
        return jnp.sum(eye * column, 0, keepdims=True)

    def to_column(row):
        return jnp.sum(eye * row, 1, keepdims=True)

    gain_t = gain[0:1, my_cols]
    gain_inv = 1.0 / gain_t
    pieces, inverses = [], []
    for i in range(4):
        squares = jnp.zeros((144, SLICE), F32)
        for n in range(NT):
            cols = slice(n * SLICE, (n + 1) * SLICE)
            hidden = in_v[i, :, cols].astype(F32) + embedded[i : i + 1, cols]
            squares = squares + hidden * hidden
        inverse = lax.rsqrt(jnp.sum(squares, -1, keepdims=True) * (1.0 / WIDTH) + NORM_EPSILON)
        hidden = in_v[i, :, my_cols].astype(F32) + embedded[i : i + 1, my_cols]
        pieces.append(hidden * inverse * gain_t)
        inverses.append(jnp.broadcast_to(inverse, (144, 128)))
    load_up.wait()
    for b in range(2):
        for r in range(4):
            rows = slice(r * SITES, (r + 1) * SITES)

            def chunk(a):
                return jnp.concatenate([a[2 * b][rows], a[2 * b + 1][rows]], 0)

            xu[b * 4 + r, 0] = chunk(pieces).astype(BF16)
            xu[b * 4 + r, 1] = jnp.concatenate(
                [up_v[2 * b].astype(F32)[rows], up_v[2 * b + 1].astype(F32)[rows]], 0
            ).astype(BF16)
            meta[b * 4 + r] = jnp.concatenate(
                [to_row(chunk(inverses)), ids[2 * b : 2 * b + 2], jnp.zeros((5, 128), F32)], 0
            )

    pl.semaphore_wait(greeted, len(peers))

    for p in range(1, NZ):
        j = mod(f + ORDER[p], NZ)
        cp.send(("z", p), xu.at[j], tok.at[yh, x, f], {"frame": j})
        cp.send(("meta", p), meta.at[j], meta_in.at[f], {"frame": j})
    local(xu.at[f], tok.at[yh, x, f], 0).wait()
    meta_in[f] = meta[f]

    def source(p):
        return mod(f - ORDER[p], NZ)

    def tokens_y(p):
        j = source(p)
        if p > 0:
            cp.arrived(("z", p), tok.at[yh, x, j], other)
            cp.arrived(("meta", p), meta_in.at[j], other)
        mine = tok.at[yh, x, j]
        cp.send(("ty", p), mine, mine, other)
        cp.send(("tr", p), mine, mine, right)
        cp.send(("tl", p), mine, mine, left)

    def tokens_x(p):
        j = source(p)
        theirs = tok.at[1 - yh, x, j]
        cp.arrived(("ty", p), theirs, other)
        cp.send(("tor", p), theirs, theirs, right)
        cp.send(("tol", p), theirs, theirs, left)

    def tokens_forward(p):
        j = source(p)
        block = tok.at[yh, xl, j]
        cp.arrived(("tr", p), block, left)
        cp.send(("tfr", p), block, block, right)
        cp.arrived(("tl", p), tok.at[yh, xr, j], right)
        block = tok.at[1 - yh, xr, j]
        cp.arrived(("tol", p), block, right)
        cp.send(("tfl", p), block, block, left)
        cp.arrived(("tor", p), tok.at[1 - yh, xl, j], left)

    def tokens_last(p):
        j = source(p)
        cp.arrived(("tfr", p), tok.at[yh, xo, j], left)
        cp.arrived(("tfl", p), tok.at[1 - yh, xo, j], right)

    def weights(step, o):
        row = yl if o == 0 else 1 - yl
        if step == 0:
            block = w_rows(f, row, c)
            if o == 0:
                for copy in load_w:
                    copy.wait()
                cp.send("wy", block, block, ypeer)
            else:
                cp.arrived("wy", block, ypeer)
            cp.send(("wu", 0, o), block, block, z_up)
            cp.send(("wd", 0, o), block, block, z_down)
            cp.send(("wc", 0, o), block, block, cpeer)
        elif step < 4:
            block = w_rows(mod(f - step, NZ), row, c)
            cp.arrived(("wu", step - 1, o), block, z_down)
            if step < 3 or o == 0:
                cp.send(("wu", step, o), block, block, z_up)
            cp.send(("wc", step, o), block, block, cpeer)
            block = w_rows(mod(f + step, NZ), row, c)
            cp.arrived(("wd", step - 1, o), block, z_up)
            if step < 3 or o == 1:
                cp.send(("wd", step, o), block, block, z_down)
            cp.send(("wc", -step, o), block, block, cpeer)
        else:
            block = w_rows(mod(f + 4, NZ), row, c)
            if o == 0:
                cp.arrived(("wu", 3, o), block, z_down)
            else:
                cp.arrived(("wd", 3, o), block, z_up)
            cp.send(("wc", 4, o), block, block, cpeer)

    def weights_last():
        for step in range(-3, 5):
            for o in range(2):
                row = yl if o == 0 else 1 - yl
                cp.arrived(("wc", step, o), w_rows(mod(f - step, NZ), row, 1 - c), cpeer)

    plan = {
        0: [(0, 0)], 1: [(0, 1)], 2: [(1, 0), (1, 1)], 4: [(2, 0), (2, 1)],
        6: [(3, 0), (3, 1)], 8: [(4, 0), (4, 1)],
    }
    for p in range(NZ + 2):
        if p < NZ:
            tokens_y(p)
        if 1 <= p <= NZ:
            tokens_x(p - 1)
        if p >= 2:
            tokens_forward(p - 2)
        for step, o in plan.get(p, ()):
            weights(step, o)
        if p == 0:
            apart = code_col[:, 0:1] - code_row[0:1, :]
            bias[...] = jnp.where((apart >= 0.0) & (apart <= 15.0), 0.0, -1e30)
    for p in range(NZ):
        tokens_last(p)
    weights_last()

    for n in range(NT):
        cols = slice(n * SLICE, (n + 1) * SLICE)
        for arr, dst in ((0, normed), (1, up)):
            dst[:, cols] = jnp.concatenate(
                [tok[n // NX, n % NX, source(p), arr].astype(F32) for p in range(NZ)], 0
            ).astype(BF16)

    @pl.loop(0, 3)
    def _(n):
        at = pl.ds(pl.multiple_of(n * 256, 256), 256)
        qkv[:, at] = nn(normed[...], wts[:, at]).astype(BF16)

    qkv[:, 768:1024] = nn(up[...], wts[:, 768:1024]).astype(BF16)

    scale = 1.0 / math.sqrt(HEAD)
    half = TOKENS // 2
    for h in range(2):
        q, k, v, g = (qkv[:, n * 256 + h * HEAD : n * 256 + (h + 1) * HEAD] for n in range(4))
        for part in range(2):
            rows = slice(part * half, (part + 1) * half)
            scores = nt(q[rows], k) * scale + bias[rows]
            exponent = jnp.exp(scores - jnp.max(scores, -1, keepdims=True))
            prob = exponent / jnp.sum(exponent, -1, keepdims=True)
            probs[rows] = prob.astype(BF16)
            grad_prob = nt(g[rows], v)
            grad_score = prob * (grad_prob - jnp.sum(grad_prob * prob, -1, keepdims=True))
            dscore[rows] = grad_score.astype(BF16)
        pb, db = probs[...], dscore[...]
        mixed[:, h * HEAD : (h + 1) * HEAD] = nn(pb, v).astype(BF16)
        grads[:, h * HEAD : (h + 1) * HEAD] = (nn(db, k) * scale).astype(BF16)
        grads[:, 256 + h * HEAD : 256 + (h + 1) * HEAD] = (tn(db, q) * scale).astype(BF16)
        grads[:, 512 + h * HEAD : 512 + (h + 1) * HEAD] = tn(pb, g).astype(BF16)

    def norm_part(plane, column):
        feature = pl.ds(pl.multiple_of((plane * NX + column) * SLICE, SLICE), SLICE)
        term = nt(grads[...], wts[feature, 0:768])
        for p in range(NZ):
            gn[plane, column, source(p)] = term[p * ROWS : (p + 1) * ROWS].astype(BF16)

    def target(p):
        return mod(f + ORDER[p], NZ)

    norm_part(0, xo)
    for p in range(NZ):
        cp.send(("a", p), gn.at[0, xo, target(p)], part_l.at[p], right)
    norm_part(1, xo)
    for p in range(NZ):
        cp.send(("b", p), gn.at[1, xo, target(p)], part_r.at[p], left)
    norm_part(1, xr)
    for p in range(NZ):
        cp.send(("c", p), gn.at[1, xr, target(p)], in_l.at[p, 1], right)
    norm_part(0, xl)
    for p in range(NZ):
        cp.send(("d", p), gn.at[0, xl, target(p)], in_r.at[p, 0], left)
    norm_part(0, xr)
    norm_part(1, xl)

    def sum_x(p):
        j = target(p)
        cp.arrived(("a", p), part_l.at[p], left)
        sum_r[p] = (gn[0, xr, j].astype(F32) + part_l[p].astype(F32)).astype(BF16)
        cp.send(("e", p), sum_r.at[p], in_l.at[p, 0], right)
        cp.arrived(("b", p), part_r.at[p], right)
        sum_l[p] = (gn[1, xl, j].astype(F32) + part_r[p].astype(F32)).astype(BF16)
        cp.send(("f", p), sum_l.at[p], in_r.at[p, 1], left)

    product = jnp.zeros((TOKENS, 128), F32)
    for n in range(6):
        cols = slice(n * 128, (n + 1) * 128)
        product = product + grads[:, cols].astype(F32) * qkv[:, cols].astype(F32)
    column = jnp.broadcast_to(jnp.sum(product, -1, keepdims=True), (TOKENS, 128))
    for p in range(NZ):
        m_part[pl.ds(source(p), 1), :] = to_row(column[p * ROWS : (p + 1) * ROWS])
    m_in[t] = m_part[...]
    for k, peer in enumerate(tensors):
        cp.send(("m", k), m_part, m_in.at[t], peer)

    for p in range(2):
        sum_x(p)
    norm_part(0, x)
    norm_part(1, x)
    for p in range(2, NZ):
        sum_x(p)

    for k, peer in enumerate(tensors):
        cp.arrived(("m", k), m_in.at[mod(t - k - 1, NT)], peer)
    row_sum = m_in[0]
    for k in range(1, NT):
        row_sum = row_sum + m_in[k]
    m_sum[...] = row_sum * (1.0 / WIDTH)
    act[...] = jnp.zeros((8, SLICE), F32)
    gterm[...] = jnp.zeros((8, SLICE), F32)

    def weight_terms(n):
        cols = slice(n * SLICE, (n + 1) * SLICE)
        term = tn(normed[:, cols], grads[...]).astype(BF16)
        term_out = tn(up[:, cols], mixed[...]).astype(BF16)
        for r in range(4):
            gw[n, r // 2, r % 2, :, 0:768] = term[64 * r : 64 * r + 64]
            gw[n, r // 2, r % 2, :, 768:1024] = term_out[64 * r : 64 * r + 64]

    def sum_y(p):
        j = target(p)
        cp.arrived(("c", p), in_l.at[p, 1], left)
        cp.arrived(("d", p), in_r.at[p, 0], right)
        cp.arrived(("e", p), in_l.at[p, 0], left)
        cp.arrived(("f", p), in_r.at[p, 1], right)
        theirs = (
            gn[1 - yh, x, j].astype(F32)
            + in_l[p, 1 - yh].astype(F32)
            + in_r[p, 1 - yh].astype(F32)
        )
        ysend[p] = theirs.astype(BF16)
        cp.send(("sy", p), ysend.at[p], yin.at[p], other)

    def to_frames(p):
        j = target(p)
        cp.arrived(("sy", p), yin.at[p], other)
        grad_norm = (
            gn[yh, x, j].astype(F32)
            + in_l[p, yh].astype(F32)
            + in_r[p, yh].astype(F32)
            + yin[p].astype(F32)
        )
        rows = tok[yh, x, j, 0].astype(F32)
        inverse = to_column(meta_in[j, 0:1, :])
        mean = to_column(m_sum[pl.ds(j, 1), :])
        grad_hidden = tok[yh, x, j, 1].astype(F32) + inverse * (
            gain_t * grad_norm - rows * (gain_inv * mean)
        )
        zsend[p] = grad_hidden.astype(BF16)
        if p == 0:
            local(zsend.at[0], full.at[yh, x, f], 0).wait()
        else:
            cp.send(("bz", p), zsend.at[p], full.at[yh, x, f], {"frame": j})
        gterm[0:1] += jnp.sum(grad_norm * rows, 0, keepdims=True)
        names = lax.broadcasted_iota(jnp.int32, (8, SLICE), 0).astype(F32)
        for fr in range(2):
            name = jnp.concatenate([meta_in[j, 1 + fr : 2 + fr, :]] * 2, 1)
            frame_sum = jnp.sum(grad_hidden[fr * SITES : (fr + 1) * SITES], 0, keepdims=True)
            act[...] += jnp.where(names == name, frame_sum, 0.0)

    def back_y(p):
        j = source(p)
        mine = full.at[yh, x, j]
        if p > 0:
            cp.arrived(("bz", p), mine, other)
        cp.send(("by", p), mine, mine, other)
        cp.send(("br", p), mine, mine, right)
        cp.send(("bl", p), mine, mine, left)

    def back_x(p):
        j = source(p)
        theirs = full.at[1 - yh, x, j]
        cp.arrived(("by", p), theirs, other)
        cp.send(("bor", p), theirs, theirs, right)
        cp.send(("bol", p), theirs, theirs, left)

    def back_forward(p):
        j = source(p)
        block = full.at[yh, xl, j]
        cp.arrived(("br", p), block, left)
        cp.send(("bfr", p), block, block, right)
        cp.arrived(("bl", p), full.at[yh, xr, j], right)
        block = full.at[1 - yh, xr, j]
        cp.arrived(("bol", p), block, right)
        cp.send(("bfl", p), block, block, left)
        cp.arrived(("bor", p), full.at[1 - yh, xl, j], left)

    def back_last(p):
        j = source(p)
        cp.arrived(("bfr", p), full.at[yh, xo, j], left)
        cp.arrived(("bfl", p), full.at[1 - yh, xo, j], right)

    def term(j, o):
        row = yl if o == 0 else 1 - yl
        return gw[j, row, c].astype(F32) + cin[j, row].astype(F32)

    def ring(step, o):
        if step == 0:
            far = mod(f + 4, NZ)
            if o == 0:
                rs_up[0, 0] = term(far, 0).astype(BF16)
                cp.send(("ru", 0, 0), rs_up.at[0, 0], ri_up.at[0, 0], z_up)
            else:
                rs_down[0, 1] = term(far, 1).astype(BF16)
                cp.send(("rd", 0, 1), rs_down.at[0, 1], ri_down.at[0, 1], z_down)
        elif step < 4:
            value = term(mod(f + 4 - step, NZ), o)
            if step > 1 or o == 0:
                cp.arrived(("ru", step - 1, o), ri_up.at[step - 1, o], z_down)
                value = value + ri_up[step - 1, o].astype(F32)
            rs_up[step, o] = value.astype(BF16)
            cp.send(("ru", step, o), rs_up.at[step, o], ri_up.at[step, o], z_up)
            value = term(mod(f - 4 + step, NZ), o)
            if step > 1 or o == 1:
                cp.arrived(("rd", step - 1, o), ri_down.at[step - 1, o], z_up)
                value = value + ri_down[step - 1, o].astype(F32)
            rs_down[step, o] = value.astype(BF16)
            cp.send(("rd", step, o), rs_down.at[step, o], ri_down.at[step, o], z_down)
        elif step == 4:
            cp.arrived(("ru", 3, o), ri_up.at[3, o], z_down)
            cp.arrived(("rd", 3, o), ri_down.at[3, o], z_up)
            value = term(f, o) + ri_up[3, o].astype(F32) + ri_down[3, o].astype(F32)
            if o == 1:
                psend[...] = value.astype(BF16)
                cp.send("py", psend, pin, ypeer)
            else:
                total_w = value
                return total_w
        return None

    def small_z_send():
        small[0:8] = act[...]
        small[8:16] = gterm[...] * gain_inv
        zin[f] = small[...]
        for k, peer in enumerate(frames):
            cp.send(("sz", k), small, zin.at[f], peer)

    def small_z_recv():
        for k, peer in enumerate(frames):
            cp.arrived(("sz", k), zin.at[mod(f - k - 1, NZ)], peer)
        acc = zin[0]
        for k in range(1, NZ):
            acc = acc + zin[k]
        sent[...] = acc
        sin[s] = acc
        for k, peer in enumerate(spaces):
            cp.send(("ss", k), sent, sin.at[s], peer)

    def small_s_recv():
        for k, peer in enumerate(spaces):
            cp.arrived(("ss", k), sin.at[mod(s - k - 1, 4)], peer)
        acc = sin[0]
        for k in range(1, 4):
            acc = acc + sin[k]
        total[...] = acc
        small_out[t] = acc
        for k, peer in enumerate(tensors):
            cp.send(("st", k), total, small_out.at[t], peer)

    def small_t_recv():
        for k, peer in enumerate(tensors):
            cp.arrived(("st", k), small_out.at[mod(t - k - 1, NT)], peer)

    def core_send():
        cp.send("core", gw.at[:, :, 1 - c], cin, cpeer)

    def core_recv():
        cp.arrived("core", cin, cpeer)

    stages = [sum_y, to_frames, back_y, back_x, back_forward]
    extra = {
        0: [lambda: [weight_terms(n) for n in (0, 1, 2, 3)]],
        1: [lambda: [weight_terms(n) for n in (4, 5, 6, 7)], core_send],
        2: [core_recv, lambda: ring(0, 0), lambda: ring(0, 1)],
        3: [lambda: ring(1, 1)],
        4: [lambda: ring(1, 0)],
        5: [lambda: ring(2, 1)],
        6: [lambda: ring(2, 0)],
        7: [lambda: ring(3, 1)],
        8: [lambda: ring(3, 0), small_z_send],
        9: [lambda: ring(4, 1), small_z_recv],
        10: [small_s_recv],
        11: [small_t_recv],
    }
    for p in range(NZ + len(stages) - 1):
        for lag, stage in enumerate(stages):
            if 0 <= p - lag < NZ:
                stage(p - lag)
        for action in extra.get(p, ()):
            action()
    own = ring(4, 0)
    cp.arrived("py", pin, ypeer)
    own = own + pin[...].astype(F32)
    for n in range(3):
        wq_sum[n] = own[:, n * 256 : (n + 1) * 256]
    wo_sum[...] = own[:, 768:1024]
    for p in range(NZ):
        back_last(p)

    for n in range(NT):
        cols = slice(n * SLICE, (n + 1) * SLICE)
        for b in range(2):
            blocks = [full[n // NX, n % NX, b * 4 + r].astype(F32) for r in range(4)]
            for fr in range(2):
                rows = slice(fr * SITES, (fr + 1) * SITES)
                out[2 * b + fr, :, cols] = jnp.concatenate(
                    [block[rows] for block in blocks], 0
                ).astype(BF16)
    cp.drain()


def on_device(inputs, upstream, action_ids, frame_time, action_table, gain, w_qkv, w_out):
    f = lax.axis_index("frame")
    actions = action_table.shape[0]
    flat_ids = action_ids.reshape(4)
    onehot = (flat_ids[:, None] == jnp.arange(actions, dtype=jnp.int32)).astype(F32)
    embedded = jnp.einsum("fa,ad->fd", onehot, action_table, precision=lax.Precision.HIGHEST)
    ids = jnp.broadcast_to(flat_ids.astype(F32)[:, None], (4, 128))

    times = lax.dynamic_index_in_dim(frame_time, f // 4, 0, keepdims=False).reshape(NZ, 2)
    times = times[(f - jnp.array(ORDER, jnp.int32)) % NZ]
    code = times[:, :, None] + 64 * jnp.arange(SITES, dtype=jnp.int32)[None, None, :]
    code = code.reshape(TOKENS).astype(F32)
    code_col = jnp.broadcast_to(code[:, None], (TOKENS, 128))
    code_row = jnp.broadcast_to(code[None, :], (8, TOKENS))

    vmem = pl.BlockSpec(memory_space=pltpu.VMEM)
    hbm = pl.BlockSpec(memory_space=pl.ANY)
    chunk = (ROWS, SLICE)
    ring_shape = (4, 2, 64, 1024)
    scratch = [
        ((4, 144, WIDTH), BF16),
        ((4, 144, SLICE), BF16),
        ((NZ, 2) + chunk, BF16),
        ((NZ, 8, 128), F32),
        ((NZ, 8, 128), F32),
        ((2, NX, NZ, 2) + chunk, BF16),
        ((WIDTH, 1024), BF16),
        ((TOKENS, WIDTH), BF16),
        ((TOKENS, WIDTH), BF16),
        ((TOKENS, TOKENS), F32),
        ((TOKENS, 1024), BF16),
        ((TOKENS, 256), BF16),
        ((TOKENS, 768), BF16),
        ((TOKENS, TOKENS), BF16),
        ((TOKENS, TOKENS), BF16),
        ((NZ, 128), F32),
        ((NT, NZ, 128), F32),
        ((NZ, 128), F32),
        ((2, NX, NZ) + chunk, BF16),
        ((NZ, 2, 2, 64, 1024), BF16),
        ((NZ,) + chunk, BF16),
        ((NZ,) + chunk, BF16),
        ((NZ,) + chunk, BF16),
        ((NZ,) + chunk, BF16),
        ((NZ, 2) + chunk, BF16),
        ((NZ, 2) + chunk, BF16),
        ((NZ,) + chunk, BF16),
        ((NZ,) + chunk, BF16),
        ((NZ,) + chunk, BF16),
        ((NZ, 2, 64, 1024), BF16),
        (ring_shape, BF16),
        (ring_shape, BF16),
        (ring_shape, BF16),
        (ring_shape, BF16),
        ((64, 1024), BF16),
        ((64, 1024), BF16),
        ((2, NX, NZ) + chunk, BF16),
        ((8, SLICE), F32),
        ((8, SLICE), F32),
        ((16, SLICE), F32),
        ((NZ, 16, SLICE), F32),
        ((16, SLICE), F32),
        ((4, 16, SLICE), F32),
        ((16, SLICE), F32),
    ]
    grad_inputs, wq_sum, wo_sum, sums = pl.pallas_call(
        kernel,
        out_shape=(
            jax.ShapeDtypeStruct((4, 144, WIDTH), BF16),
            jax.ShapeDtypeStruct((3, 64, 256), F32),
            jax.ShapeDtypeStruct((64, 256), F32),
            jax.ShapeDtypeStruct((NT, 16, SLICE), F32),
        ),
        in_specs=[hbm] * 4 + [vmem] * 5,
        out_specs=(vmem,) * 4,
        scratch_shapes=[pltpu.VMEM(shape, kind) for shape, kind in scratch]
        + [
            pltpu.SemaphoreType.DMA((SLOTS,)),
            pltpu.SemaphoreType.DMA((SLOTS,)),
            pltpu.SemaphoreType.DMA((6,)),
        ],
        compiler_params=pltpu.CompilerParams(
            collective_id=0, has_side_effects=True, vmem_limit_bytes=VMEM_BYTES
        ),
    )(
        inputs.reshape(4, 144, WIDTH),
        upstream.reshape(4, 144, WIDTH),
        w_qkv.transpose(1, 0, 2),
        w_out,
        embedded,
        ids,
        gain.reshape(1, WIDTH),
        code_col,
        code_row,
    )
    sums = sums.transpose(1, 0, 2).reshape(16, WIDTH)
    return (
        grad_inputs.reshape(inputs.shape),
        wq_sum.transpose(1, 0, 2),
        wo_sum,
        sums[8],
        sums[:8],
    )


def solution(mesh):
    return jax.shard_map(
        on_device,
        mesh=mesh,
        in_specs=(
            P(None, "frame", "space", None),
            P(None, "frame", "space", None),
            P(None, "frame"),
            P(),
            P(),
            P(),
            P(("frame", "space"), None, "tensor"),
            P(("frame", "space"), "tensor"),
        ),
        out_specs=(
            P(None, "frame", "space", None),
            P(("frame", "space"), None, "tensor"),
            P(("frame", "space"), "tensor"),
            P(),
            P(),
        ),
        check_vma=False,
    )
```

time: 811 us -> 160 us (0.20)
  waiting for transfers between devices: 605 us -> 0 us
  Pallas kernels: 0 us -> 145 us
  blocking collectives: 96.5 us -> 0 us
  matrix products: 31 us -> 0.84 us
  local copies, waits for them, and re-layouts: 32.4 us -> 11.9 us
  other arithmetic: 17 us -> 0.76 us
  between operations: 14.4 us -> 0.69 us
  starting transfers between devices: 11.1 us -> 0 us
    psum x2 -> x0, waiting for transfers between devices: 293 us -> none  [the longest x1 197 us: on_device(): lax.psum((gain_term, action_term), ('frame', 'space'))]
    pallas_call x0 -> x1, Pallas kernels: none -> 145 us  [on_device(): pl.pallas_call(kernel, out_shape=(jax.ShapeDtypeStruct((4, 144, WIDTH), B...]
    reduce_scatter x1 -> x0, waiting for transfers between devices: 126 us -> none  [on_device(): lax.psum_scatter(term_qkv, ('frame', 'space'), scatter_dimension=0, tiled...]
    all_gather x2 -> x0, waiting for transfers between devices: 121 us -> none  [the longest x1 60.6 us: on_device(): full_qkv = lax.all_gather(w_qkv, ('frame', 'space'), axis=0, tiled=True)]
    psum x1 -> x0, blocking collectives: 54.9 us -> none  [on_device(): lax.psum((gain_term, action_term), ('frame', 'space'))]
    unnamed x7 -> x0, waiting for transfers between devices: 43.6 us -> none
    all_to_all x2 -> x0, blocking collectives: 41.7 us -> none  [the longest x1 28.4 us: on_device(): lax.all_to_all(grad_merged, 'frame', split_axis=1, concat_axis=2, tiled=T...]
    dot_general x12 -> x1, matrix products: 28.6 us -> 0.84 us  [on_device(): jnp.einsum('fa,ad->fd', onehot, action_table, precision=lax.Precision.HIG...]
  transfers between devices with their start and end apart: 8 -> 0, of which waited for: 7 -> 0; matrix products, arithmetic and copies ran while one was open for 6% -> 0% of each run, Pallas kernels for 0% -> 0%
where the time goes in v2:
time: 160 us
  Pallas kernels  145 us (91%)
  local copies, waits for them, and re-layouts  11.9 us (7%)
    pallas_call x1, Pallas kernels, on_device(): pl.pallas_call(kernel, out_shape=(jax.ShapeDtypeStruct((4, 144, WIDTH), B...  145 us
    unnamed x9, local copies, waits for them, and re-layouts  4.72 us

profile of v2, /device:TPU:1, one launch (start us, length us, event | category | flops | bytes accessed | tf_op | source)
XLA Modules:
  0.0 159.7 jit_solution(13695687942737440190)
XLA Ops:
  0.6 0.0 copy-start
  0.7 0.7 compare_select_fusion
  1.3 0.7 dynamic-slice_reduce_fusion
  2.0 0.8 eq.17
  2.8 0.6 broadcast_in_dim.8.ids
  3.5 0.1 reshape.71
  3.5 0.6 gather_fusion
  4.1 0.1 add_convert_fusion
  4.2 0.1 convert_element_type.24
  4.3 0.6 broadcast_in_dim.11.code_row
  4.9 0.0 copy-done
  4.9 0.8 fusion.embedded
  5.7 0.9 broadcast_in_dim.10.code_col
  6.6 145.5 %shard_map.128 = (bf16[4,144,2048]{2,1,0:T(8,128)(2,1)}, f32[3,64,256]{2,1,0:T(8,128)}, f32[64,256]{1,0:T(8,128)}, f32[8,16,256]{2,1,0:T(8,128)}) custom-call(bf16[4,144,2048]{2,1,0:T(8,128)(2,1)} %bitcast.10, bf16[4,144,2048]{2,1,0:T(8,128)(2,1)} %bitcast.11, bf16[3,64,256]{2,1,0:T(8,128)(2,1)} %bitcast.14, bf16[64,256]{1,0:T(8,128)(2,1)} %wo.1, ...), custom_call_target="tpu_custom_call" | custom-call | tf_op jit(solution)/shard_map/pallas_call | solution.py:626
  152.1 1.4 slice.15
  153.5 1.5 slice.16
  155.0 0.0 copy-start.1
  155.0 0.0 copy-start.2
  155.0 3.4 %copy.17 = bf16[2,2,144,2048]{3,2,1,0:T(8,128)(2,1)} copy(bf16[2,2,144,2048]{3,2,1,0:T(8,128)(2,1)} %bitcast.12) | data formatting | bytes 4718592
  158.4 0.0 copy-done.1
  158.4 0.7 copy.18
  159.1 0.0 copy-done.2
  159.1 0.6 copy.19
  (3 shorter events, 0.0 us)
Async XLA Ops:
  0.6 4.3 %copy-start = (f32[8,2048]{1,0:T(8,128)S(1)}, f32[8,2048]{1,0:T(8,128)}, u32[]{:S(2)}) copy-start(f32[8,2048]{1,0:T(8,128)} %param.13) | copy-start | bytes 196612
  155.0 3.4 %copy-start.1 = (f32[3,64,256]{2,1,0:T(8,128)S(1)}, f32[3,64,256]{2,1,0:T(8,128)}, u32[]{:S(2)}) copy-start(f32[3,64,256]{2,1,0:T(8,128)} %get-tuple-element.10) | copy-start | bytes 589828
  155.0 4.1 %copy-start.2 = (f32[64,256]{1,0:T(8,128)S(1)}, f32[64,256]{1,0:T(8,128)}, u32[]{:S(2)}) copy-start(f32[64,256]{1,0:T(8,128)} %get-tuple-element.20) | copy-start | bytes 196612

commit v3 on v2

--- a/solution.py
+++ b/solution.py
@@ -21,7 +21,28 @@
 WIDTH = 2048
 VMEM_BYTES = 58 * 1024 * 1024
 ORDER = (0, 1, 7, 2, 6, 3, 5, 4)
-SLOTS = 320
+SLOTS = 400
+ACROSS = (3, 4, 5, 6, 7)
+GATHER = (
+    ("w", 0, 0), ("zsend",), ("t0a", 0), ("t1a", 0), ("t1b", 0), ("w", 0, 1), ("w", 1, 0), ("t1c", 0),
+    ("t0b", 0), ("t0a", 1), ("t1a", 1), ("t0a", 2), ("t1a", 2), ("t0c", 0), ("t0b", 1), ("t0a", 3),
+    ("t1a", 3), ("t0a", 4), ("t1a", 4), ("t1b", 1), ("t1c", 1), ("t0b", 2), ("t1b", 2), ("t0b", 3),
+    ("t1c", 2), ("t0b", 4), ("t0a", 5), ("t1a", 5), ("t0a", 6), ("t1a", 6), ("t0c", 1), ("t1b", 3),
+    ("t1c", 3), ("t0a", 7), ("t1a", 7), ("t1b", 4), ("t1c", 4), ("w", 1, 1), ("t0c", 2), ("t0b", 5),
+    ("t0c", 3), ("t0c", 4), ("t0b", 6), ("w", 2, 0), ("t1b", 5), ("t1c", 5), ("t1b", 6), ("w", 2, 1),
+    ("t0b", 7), ("t1c", 6), ("rp", 0), ("w", 3, 0), ("t1b", 7), ("t1c", 7), ("t0c", 5), ("w", 3, 1),
+    ("rp", 1), ("t0c", 6), ("w", 4, 0), ("t0c", 7), ("rp", 2), ("w", 4, 1),
+)
+REDUCE = (
+    ("np", 0), ("np0s",), ("np", 1), ("ra", 0), ("ra", 1), ("ra", 2), ("m",), ("wt", 0), ("wt", 1), ("wt", 2),
+    ("rx", 0), ("rx", 3), ("wt", 3), ("rg", 0), ("rx", 1), ("wt", 4), ("wt", 5), ("rx", 2), ("rx", 4),
+    ("wt", 6), ("sy", 0), ("wt", 7), ("tf", 3), ("rg", 1, 0), ("rg", 1, 1), ("rx", 5), ("sy", 1), ("sy", 2),
+    ("tf", 4), ("rx", 6), ("ba", 3), ("tf", 5), ("rx", 7), ("rg", 2, 0), ("tf", 0), ("ba", 0), ("tf", 6),
+    ("tf", 1), ("tf", 2), ("bb", 3), ("rg", 2, 1), ("ba", 4), ("tf", 7), ("bb", 0), ("s0",), ("ba", 5),
+    ("bc", 3), ("bb", 4), ("bc", 0), ("rg", 3, 0), ("bb", 5), ("ba", 6), ("ba", 1), ("ba", 2), ("bc", 4),
+    ("bc", 5), ("bb", 6), ("rg", 3, 1), ("bb", 1), ("bb", 2), ("ba", 7), ("s1",), ("bc", 6), ("bb", 7),
+    ("s2",), ("bc", 1), ("bc", 2), ("rg", 4, 1), ("bc", 7), ("rg", 4, 0),
+)
 
 
 def mod(value, n):
@@ -78,11 +99,11 @@
 
 
 def kernel(
-    inputs, upstream, w3, wo, embedded, ids, gain, code_col, code_row,
-    out, wq_sum, wo_sum, small_out,
-    in_v, up_v, xu, meta, meta_in, tok, wts, normed, up, bias, qkv, mixed, grads, probs, dscore,
+    inputs, upstream, w3, wo, ids, times, table, gain,
+    out, wq_sum, wo_sum, gain_out, act_out,
+    in_v, up_v, embedded, xu, meta, meta_in, tok, wts, normed, up, bias, qkv, mixed, grads, probs, dscore,
     m_part, m_in, m_sum, gn, gw, part_l, part_r, sum_l, sum_r, in_l, in_r, ysend, yin, zsend,
-    cin, rs_up, rs_down, ri_up, ri_down, psend, pin, full,
+    cin, rs_up, rs_down, ri_up, ri_down, psend, pin, full, ry, rsend, rin, small_out,
     act, gterm, small, zin, sent, sin, total,
     send_sems, recv_sems, local_sems,
 ):
@@ -93,6 +114,7 @@
     xl, xr, xo = mod(x - 1, NX), mod(x + 1, NX), mod(x + 2, NX)
     right, left = {"tensor": yh * NX + xr}, {"tensor": yh * NX + xl}
     other = {"tensor": (1 - yh) * NX + x}
+    opposite = {"tensor": yh * NX + xo}
     z_up, z_down = {"frame": mod(f + 1, NZ)}, {"frame": mod(f - 1, NZ)}
     ypeer = {"space": (1 - yl) * 2 + c}
     cpeer = {"space": yl * 2 + 1 - c}
@@ -122,6 +144,35 @@
     load_w = [
         local(w3.at[n], wts.at[own_rows, n * 256 : (n + 1) * 256], 2 + n) for n in range(3)
     ] + [local(wo, wts.at[own_rows, 768:1024], 5)]
+
+    def source(p):
+        return mod(f - ORDER[p], NZ)
+
+    def target(p):
+        return mod(f + ORDER[p], NZ)
+
+    spot = lax.broadcasted_iota(jnp.int32, (ROWS, 128), 0)
+    lane = lax.broadcasted_iota(jnp.int32, (8, TOKENS), 1)
+    columns = []
+    time_row = jnp.zeros((8, TOKENS), jnp.int32)
+    for p in range(NZ):
+        pair = [times[f // 4, 2 * source(p) + fr] for fr in range(2)]
+        second = spot >= SITES
+        columns.append(jnp.where(second, pair[1] + 64 * (spot - SITES), pair[0] + 64 * spot))
+        for fr in range(2):
+            start = p * ROWS + fr * SITES
+            time_row = jnp.where((lane >= start) & (lane < start + SITES), pair[fr], time_row)
+    site_row = lax.rem(lane, SITES)
+    code_col = jnp.concatenate(columns, 0)[:, 0:1]
+    code_row = (time_row + 64 * site_row)[0:1, :]
+    apart = code_col - code_row
+    bias[...] = jnp.where((apart >= 0) & (apart <= 15), 0.0, -1e30)
+
+    names = lax.broadcasted_iota(jnp.int32, (8, WIDTH), 0)
+    for i in range(4):
+        embedded[i : i + 1] = jnp.sum(
+            jnp.where(names == ids[i], table[...], 0.0), 0, keepdims=True
+        )
     load_in.wait()
 
     lane = lax.broadcasted_iota(jnp.int32, (ROWS, 128), 1)
@@ -159,53 +210,91 @@
                 [up_v[2 * b].astype(F32)[rows], up_v[2 * b + 1].astype(F32)[rows]], 0
             ).astype(BF16)
             meta[b * 4 + r] = jnp.concatenate(
-                [to_row(chunk(inverses)), ids[2 * b : 2 * b + 2], jnp.zeros((5, 128), F32)], 0
+                [to_row(chunk(inverses))]
+                + [jnp.full((1, 128), ids[2 * b + fr].astype(F32), F32) for fr in range(2)]
+                + [jnp.zeros((5, 128), F32)],
+                0,
             )
 
     pl.semaphore_wait(greeted, len(peers))
 
-    for p in range(1, NZ):
-        j = mod(f + ORDER[p], NZ)
-        cp.send(("z", p), xu.at[j], tok.at[yh, x, f], {"frame": j})
-        cp.send(("meta", p), meta.at[j], meta_in.at[f], {"frame": j})
-    local(xu.at[f], tok.at[yh, x, f], 0).wait()
-    meta_in[f] = meta[f]
-
-    def source(p):
-        return mod(f - ORDER[p], NZ)
-
-    def tokens_y(p):
+    def tokens_send():
+        for p in range(1, NZ):
+            j = target(p)
+            cp.send(("z", p), xu.at[j], tok.at[yh, x, f], {"frame": j})
+            cp.send(("meta", p), meta.at[j], meta_in.at[f], {"frame": j})
+        local(xu.at[f], tok.at[yh, x, f], 0).wait()
+        meta_in[f] = meta[f]
+
+    def normed_a(p):
         j = source(p)
         if p > 0:
             cp.arrived(("z", p), tok.at[yh, x, j], other)
             cp.arrived(("meta", p), meta_in.at[j], other)
-        mine = tok.at[yh, x, j]
-        cp.send(("ty", p), mine, mine, other)
-        cp.send(("tr", p), mine, mine, right)
-        cp.send(("tl", p), mine, mine, left)
-
-    def tokens_x(p):
+        mine = tok.at[yh, x, j, 0]
+        cp.send(("t0y", p), mine, mine, other)
+        cp.send(("t0r", p), mine, mine, right)
+        cp.send(("t0l", p), mine, mine, left)
+
+    def normed_b(p):
+        theirs = tok.at[1 - yh, x, source(p), 0]
+        cp.arrived(("t0y", p), theirs, other)
+        cp.send(("t0or", p), theirs, theirs, right)
+        cp.send(("t0ol", p), theirs, theirs, left)
+
+    def normed_c(p):
         j = source(p)
-        theirs = tok.at[1 - yh, x, j]
-        cp.arrived(("ty", p), theirs, other)
-        cp.send(("tor", p), theirs, theirs, right)
-        cp.send(("tol", p), theirs, theirs, left)
-
-    def tokens_forward(p):
+        block = tok.at[yh, xl, j, 0]
+        cp.arrived(("t0r", p), block, left)
+        cp.send(("t0fr", p), block, block, right)
+        block = tok.at[1 - yh, xr, j, 0]
+        cp.arrived(("t0ol", p), block, right)
+        cp.send(("t0fl", p), block, block, left)
+
+    def upstream_a(p):
+        mine = tok.at[yh, x, source(p), 1]
+        cp.send(("t1r", p), mine, mine, right)
+        cp.send(("t1l", p), mine, mine, left)
+        cp.send(("t1y", p), mine, mine, other)
+        cp.send(("t1o", p), mine, mine, opposite)
+
+    def upstream_b(p):
         j = source(p)
-        block = tok.at[yh, xl, j]
-        cp.arrived(("tr", p), block, left)
-        cp.send(("tfr", p), block, block, right)
-        cp.arrived(("tl", p), tok.at[yh, xr, j], right)
-        block = tok.at[1 - yh, xr, j]
-        cp.arrived(("tol", p), block, right)
-        cp.send(("tfl", p), block, block, left)
-        cp.arrived(("tor", p), tok.at[1 - yh, xl, j], left)
+        for name, at, device in ((("t1r", p), xl, left), (("t1l", p), xr, right)):
+            block = tok.at[yh, at, j, 1]
+            cp.arrived(name, block, device)
+            cp.send((name, "y"), block, block, other)
+
+    def upstream_c(p):
+        block = tok.at[yh, xo, source(p), 1]
+        cp.arrived(("t1o", p), block, opposite)
+        cp.send(("t1oy", p), block, block, other)
 
     def tokens_last(p):
         j = source(p)
-        cp.arrived(("tfr", p), tok.at[yh, xo, j], left)
-        cp.arrived(("tfl", p), tok.at[1 - yh, xo, j], right)
+        cp.arrived(("t0l", p), tok.at[yh, xr, j, 0], right)
+        cp.arrived(("t0or", p), tok.at[1 - yh, xl, j, 0], left)
+        cp.arrived(("t0fr", p), tok.at[yh, xo, j, 0], left)
+        cp.arrived(("t0fl", p), tok.at[1 - yh, xo, j, 0], right)
+        cp.arrived(("t1y", p), tok.at[1 - yh, x, j, 1], other)
+        cp.arrived((("t1r", p), "y"), tok.at[1 - yh, xl, j, 1], other)
+        cp.arrived((("t1l", p), "y"), tok.at[1 - yh, xr, j, 1], other)
+        cp.arrived(("t1oy", p), tok.at[1 - yh, xo, j, 1], other)
+
+    def repack(pair):
+        for p in (2 * pair, 2 * pair + 1):
+            tokens_last(p)
+        rows = slice(pair * 2 * ROWS, (pair + 1) * 2 * ROWS)
+        for n in range(NT):
+            cols = slice(n * SLICE, (n + 1) * SLICE)
+            for arr, dst in ((0, normed), (1, up)):
+                dst[rows, cols] = jnp.concatenate(
+                    [
+                        tok[n // NX, n % NX, source(p), arr].astype(F32)
+                        for p in (2 * pair, 2 * pair + 1)
+                    ],
+                    0,
+                ).astype(BF16)
 
     def weights(step, o):
         row = yl if o == 0 else 1 - yl
@@ -245,32 +334,14 @@
                 row = yl if o == 0 else 1 - yl
                 cp.arrived(("wc", step, o), w_rows(mod(f - step, NZ), row, 1 - c), cpeer)
 
-    plan = {
-        0: [(0, 0)], 1: [(0, 1)], 2: [(1, 0), (1, 1)], 4: [(2, 0), (2, 1)],
-        6: [(3, 0), (3, 1)], 8: [(4, 0), (4, 1)],
+    actions = {
+        "w": weights, "zsend": tokens_send, "t0a": normed_a, "t0b": normed_b, "t0c": normed_c,
+        "t1a": upstream_a, "t1b": upstream_b, "t1c": upstream_c, "rp": repack,
     }
-    for p in range(NZ + 2):
-        if p < NZ:
-            tokens_y(p)
-        if 1 <= p <= NZ:
-            tokens_x(p - 1)
-        if p >= 2:
-            tokens_forward(p - 2)
-        for step, o in plan.get(p, ()):
-            weights(step, o)
-        if p == 0:
-            apart = code_col[:, 0:1] - code_row[0:1, :]
-            bias[...] = jnp.where((apart >= 0.0) & (apart <= 15.0), 0.0, -1e30)
-    for p in range(NZ):
-        tokens_last(p)
+    for name, *where in GATHER:
+        actions[name](*where)
+    repack(3)
     weights_last()
-
-    for n in range(NT):
-        cols = slice(n * SLICE, (n + 1) * SLICE)
-        for arr, dst in ((0, normed), (1, up)):
-            dst[:, cols] = jnp.concatenate(
-                [tok[n // NX, n % NX, source(p), arr].astype(F32) for p in range(NZ)], 0
-            ).astype(BF16)
 
     @pl.loop(0, 3)
     def _(n):
@@ -304,91 +375,111 @@
         for p in range(NZ):
             gn[plane, column, source(p)] = term[p * ROWS : (p + 1) * ROWS].astype(BF16)
 
-    def target(p):
-        return mod(f + ORDER[p], NZ)
-
-    norm_part(0, xo)
-    for p in range(NZ):
-        cp.send(("a", p), gn.at[0, xo, target(p)], part_l.at[p], right)
-    norm_part(1, xo)
-    for p in range(NZ):
-        cp.send(("b", p), gn.at[1, xo, target(p)], part_r.at[p], left)
-    norm_part(1, xr)
-    for p in range(NZ):
-        cp.send(("c", p), gn.at[1, xr, target(p)], in_l.at[p, 1], right)
-    norm_part(0, xl)
-    for p in range(NZ):
-        cp.send(("d", p), gn.at[0, xl, target(p)], in_r.at[p, 0], left)
-    norm_part(0, xr)
-    norm_part(1, xl)
-
-    def sum_x(p):
+    def norm_parts(which):
+        plane = 1 - yh if which == 0 else yh
+        for column in range(NX):
+            norm_part(plane, column)
+
+    def send_across():
+        for p in ACROSS:
+            cp.send(("ry", p), gn.at[1 - yh, :, target(p)], ry.at[p], other)
+
+    def reduce_a(p):
         j = target(p)
+        cp.send(("a", p), gn.at[1 - yh, xo, j], part_l.at[p], right)
+        cp.send(("b", p), gn.at[yh, xo, j], part_r.at[p], left)
+        cp.send(("c", p), gn.at[yh, xr, j], in_l.at[p, 0], right)
+        cp.send(("d", p), gn.at[1 - yh, xl, j], in_r.at[p, 1], left)
+
+    def reduce_x(p):
+        j = target(p)
+        if p in ACROSS:
+            cp.arrived(("ry", p), ry.at[p], other)
+            for i, (column, device) in enumerate(((xr, right), (xl, left), (xo, opposite))):
+                rsend[p, i] = (
+                    gn[yh, column, j].astype(F32) + ry[p, column].astype(F32)
+                ).astype(BF16)
+                cp.send(("rx", p, i), rsend.at[p, i], rin.at[p, i], device)
+            return
         cp.arrived(("a", p), part_l.at[p], left)
-        sum_r[p] = (gn[0, xr, j].astype(F32) + part_l[p].astype(F32)).astype(BF16)
-        cp.send(("e", p), sum_r.at[p], in_l.at[p, 0], right)
+        sum_r[p] = (gn[1 - yh, xr, j].astype(F32) + part_l[p].astype(F32)).astype(BF16)
+        cp.send(("e", p), sum_r.at[p], in_l.at[p, 1], right)
         cp.arrived(("b", p), part_r.at[p], right)
-        sum_l[p] = (gn[1, xl, j].astype(F32) + part_r[p].astype(F32)).astype(BF16)
-        cp.send(("f", p), sum_l.at[p], in_r.at[p, 1], left)
-
-    product = jnp.zeros((TOKENS, 128), F32)
-    for n in range(6):
-        cols = slice(n * 128, (n + 1) * 128)
-        product = product + grads[:, cols].astype(F32) * qkv[:, cols].astype(F32)
-    column = jnp.broadcast_to(jnp.sum(product, -1, keepdims=True), (TOKENS, 128))
-    for p in range(NZ):
-        m_part[pl.ds(source(p), 1), :] = to_row(column[p * ROWS : (p + 1) * ROWS])
-    m_in[t] = m_part[...]
-    for k, peer in enumerate(tensors):
-        cp.send(("m", k), m_part, m_in.at[t], peer)
-
-    for p in range(2):
-        sum_x(p)
-    norm_part(0, x)
-    norm_part(1, x)
-    for p in range(2, NZ):
-        sum_x(p)
-
-    for k, peer in enumerate(tensors):
-        cp.arrived(("m", k), m_in.at[mod(t - k - 1, NT)], peer)
-    row_sum = m_in[0]
-    for k in range(1, NT):
-        row_sum = row_sum + m_in[k]
-    m_sum[...] = row_sum * (1.0 / WIDTH)
-    act[...] = jnp.zeros((8, SLICE), F32)
-    gterm[...] = jnp.zeros((8, SLICE), F32)
-
-    def weight_terms(n):
-        cols = slice(n * SLICE, (n + 1) * SLICE)
+        sum_l[p] = (gn[yh, xl, j].astype(F32) + part_r[p].astype(F32)).astype(BF16)
+        cp.send(("f", p), sum_l.at[p], in_r.at[p, 0], left)
+
+    def send_means():
+        product = jnp.zeros((TOKENS, 128), F32)
+        for n in range(6):
+            cols = slice(n * 128, (n + 1) * 128)
+            product = product + grads[:, cols].astype(F32) * qkv[:, cols].astype(F32)
+        column = jnp.broadcast_to(jnp.sum(product, -1, keepdims=True), (TOKENS, 128))
+        for p in range(NZ):
+            m_part[pl.ds(source(p), 1), :] = to_row(column[p * ROWS : (p + 1) * ROWS])
+        m_in[t] = m_part[...]
+        for k, peer in enumerate(tensors):
+            cp.send(("m", k), m_part, m_in.at[t], peer)
+
+    def take_means():
+        for k, peer in enumerate(tensors):
+            cp.arrived(("m", k), m_in.at[mod(t - k - 1, NT)], peer)
+        row_sum = m_in[0]
+        for k in range(1, NT):
+            row_sum = row_sum + m_in[k]
+        m_sum[...] = row_sum * (1.0 / WIDTH)
+        act[...] = jnp.zeros((8, SLICE), F32)
+        gterm[...] = jnp.zeros((8, SLICE), F32)
+
+    blocks = [mod(f + k, NZ) for k in (4, 3, -3, 2, -2, 1, -1, 0)]
+    shared = set()
+
+    def weight_terms(i):
+        n = blocks[i]
+        cols = pl.ds(pl.multiple_of(n * SLICE, SLICE), SLICE)
         term = tn(normed[:, cols], grads[...]).astype(BF16)
         term_out = tn(up[:, cols], mixed[...]).astype(BF16)
         for r in range(4):
             gw[n, r // 2, r % 2, :, 0:768] = term[64 * r : 64 * r + 64]
             gw[n, r // 2, r % 2, :, 768:1024] = term_out[64 * r : 64 * r + 64]
+        cp.send(("core", i), gw.at[n, :, 1 - c], cin.at[n], cpeer)
+
+    def partner_terms(*which):
+        for i in which:
+            if i not in shared:
+                shared.add(i)
+                cp.arrived(("core", i), cin.at[blocks[i]], cpeer)
 
     def sum_y(p):
         j = target(p)
-        cp.arrived(("c", p), in_l.at[p, 1], left)
-        cp.arrived(("d", p), in_r.at[p, 0], right)
-        cp.arrived(("e", p), in_l.at[p, 0], left)
-        cp.arrived(("f", p), in_r.at[p, 1], right)
+        cp.arrived(("c", p), in_l.at[p, 0], left)
+        cp.arrived(("d", p), in_r.at[p, 1], right)
+        cp.arrived(("e", p), in_l.at[p, 1], left)
+        cp.arrived(("f", p), in_r.at[p, 0], right)
         theirs = (
-            gn[1 - yh, x, j].astype(F32)
-            + in_l[p, 1 - yh].astype(F32)
-            + in_r[p, 1 - yh].astype(F32)
+            gn[1 - yh, x, j].astype(F32) + in_l[p, 1].astype(F32) + in_r[p, 1].astype(F32)
         )
         ysend[p] = theirs.astype(BF16)
         cp.send(("sy", p), ysend.at[p], yin.at[p], other)
 
     def to_frames(p):
         j = target(p)
-        cp.arrived(("sy", p), yin.at[p], other)
-        grad_norm = (
-            gn[yh, x, j].astype(F32)
-            + in_l[p, yh].astype(F32)
-            + in_r[p, yh].astype(F32)
-            + yin[p].astype(F32)
-        )
+        if not shared.issuperset(("mean",)):
+            shared.add("mean")
+            take_means()
+        grad_norm = gn[yh, x, j].astype(F32)
+        if p in ACROSS:
+            for i, device in enumerate((left, right, opposite)):
+                cp.arrived(("rx", p, i), rin.at[p, i], device)
+                grad_norm = grad_norm + rin[p, i].astype(F32)
+            grad_norm = grad_norm + ry[p, x].astype(F32)
+        else:
+            cp.arrived(("sy", p), yin.at[p], other)
+            grad_norm = (
+                grad_norm
+                + in_l[p, 0].astype(F32)
+                + in_r[p, 0].astype(F32)
+                + yin[p].astype(F32)
+            )
         rows = tok[yh, x, j, 0].astype(F32)
         inverse = to_column(meta_in[j, 0:1, :])
         mean = to_column(m_sum[pl.ds(j, 1), :])
@@ -401,11 +492,11 @@
         else:
             cp.send(("bz", p), zsend.at[p], full.at[yh, x, f], {"frame": j})
         gterm[0:1] += jnp.sum(grad_norm * rows, 0, keepdims=True)
-        names = lax.broadcasted_iota(jnp.int32, (8, SLICE), 0).astype(F32)
+        labels = lax.broadcasted_iota(jnp.int32, (8, SLICE), 0).astype(F32)
         for fr in range(2):
             name = jnp.concatenate([meta_in[j, 1 + fr : 2 + fr, :]] * 2, 1)
             frame_sum = jnp.sum(grad_hidden[fr * SITES : (fr + 1) * SITES], 0, keepdims=True)
-            act[...] += jnp.where(names == name, frame_sum, 0.0)
+            act[...] += jnp.where(labels == name, frame_sum, 0.0)
 
     def back_y(p):
         j = source(p)
@@ -428,14 +519,14 @@
         block = full.at[yh, xl, j]
         cp.arrived(("br", p), block, left)
         cp.send(("bfr", p), block, block, right)
-        cp.arrived(("bl", p), full.at[yh, xr, j], right)
         block = full.at[1 - yh, xr, j]
         cp.arrived(("bol", p), block, right)
         cp.send(("bfl", p), block, block, left)
-        cp.arrived(("bor", p), full.at[1 - yh, xl, j], left)
 
     def back_last(p):
         j = source(p)
+        cp.arrived(("bl", p), full.at[yh, xr, j], right)
+        cp.arrived(("bor", p), full.at[1 - yh, xl, j], left)
         cp.arrived(("bfr", p), full.at[yh, xo, j], left)
         cp.arrived(("bfl", p), full.at[1 - yh, xo, j], right)
 
@@ -443,39 +534,42 @@
         row = yl if o == 0 else 1 - yl
         return gw[j, row, c].astype(F32) + cin[j, row].astype(F32)
 
-    def ring(step, o):
+    def ring(step, o=None):
         if step == 0:
-            far = mod(f + 4, NZ)
-            if o == 0:
-                rs_up[0, 0] = term(far, 0).astype(BF16)
-                cp.send(("ru", 0, 0), rs_up.at[0, 0], ri_up.at[0, 0], z_up)
-            else:
-                rs_down[0, 1] = term(far, 1).astype(BF16)
-                cp.send(("rd", 0, 1), rs_down.at[0, 1], ri_down.at[0, 1], z_down)
+            partner_terms(0)
+            far = blocks[0]
+            rs_up[0, 0] = term(far, 0).astype(BF16)
+            cp.send(("ru", 0, 0), rs_up.at[0, 0], ri_up.at[0, 0], z_up)
+            rs_down[0, 1] = term(far, 1).astype(BF16)
+            cp.send(("rd", 0, 1), rs_down.at[0, 1], ri_down.at[0, 1], z_down)
         elif step < 4:
-            value = term(mod(f + 4 - step, NZ), o)
+            partner_terms(2 * step - 1, 2 * step)
+            value = term(blocks[2 * step - 1], o)
             if step > 1 or o == 0:
                 cp.arrived(("ru", step - 1, o), ri_up.at[step - 1, o], z_down)
                 value = value + ri_up[step - 1, o].astype(F32)
             rs_up[step, o] = value.astype(BF16)
             cp.send(("ru", step, o), rs_up.at[step, o], ri_up.at[step, o], z_up)
-            value = term(mod(f - 4 + step, NZ), o)
+            value = term(blocks[2 * step], o)
             if step > 1 or o == 1:
                 cp.arrived(("rd", step - 1, o), ri_down.at[step - 1, o], z_up)
                 value = value + ri_down[step - 1, o].astype(F32)
             rs_down[step, o] = value.astype(BF16)
             cp.send(("rd", step, o), rs_down.at[step, o], ri_down.at[step, o], z_down)
-        elif step == 4:
+        else:
+            partner_terms(7)
             cp.arrived(("ru", 3, o), ri_up.at[3, o], z_down)
             cp.arrived(("rd", 3, o), ri_down.at[3, o], z_up)
             value = term(f, o) + ri_up[3, o].astype(F32) + ri_down[3, o].astype(F32)
             if o == 1:
                 psend[...] = value.astype(BF16)
                 cp.send("py", psend, pin, ypeer)
-            else:
-                total_w = value
-                return total_w
-        return None
+                return
+            cp.arrived("py", pin, ypeer)
+            value = value + pin[...].astype(F32)
+            for n in range(3):
+                wq_sum[n] = value[:, n * 256 : (n + 1) * 256]
+            wo_sum[...] = value[:, 768:1024]
 
     def small_z_send():
         small[0:8] = act[...]
@@ -510,39 +604,18 @@
         for k, peer in enumerate(tensors):
             cp.arrived(("st", k), small_out.at[mod(t - k - 1, NT)], peer)
 
-    def core_send():
-        cp.send("core", gw.at[:, :, 1 - c], cin, cpeer)
-
-    def core_recv():
-        cp.arrived("core", cin, cpeer)
-
-    stages = [sum_y, to_frames, back_y, back_x, back_forward]
-    extra = {
-        0: [lambda: [weight_terms(n) for n in (0, 1, 2, 3)]],
-        1: [lambda: [weight_terms(n) for n in (4, 5, 6, 7)], core_send],
-        2: [core_recv, lambda: ring(0, 0), lambda: ring(0, 1)],
-        3: [lambda: ring(1, 1)],
-        4: [lambda: ring(1, 0)],
-        5: [lambda: ring(2, 1)],
-        6: [lambda: ring(2, 0)],
-        7: [lambda: ring(3, 1)],
-        8: [lambda: ring(3, 0), small_z_send],
-        9: [lambda: ring(4, 1), small_z_recv],
-        10: [small_s_recv],
-        11: [small_t_recv],
+    actions = {
+        "np": norm_parts, "np0s": send_across, "ra": reduce_a, "rx": reduce_x, "m": send_means,
+        "wt": weight_terms, "rg": ring, "sy": sum_y, "tf": to_frames, "ba": back_y, "bb": back_x,
+        "bc": back_forward, "s0": small_z_send, "s1": small_z_recv, "s2": small_s_recv,
     }
-    for p in range(NZ + len(stages) - 1):
-        for lag, stage in enumerate(stages):
-            if 0 <= p - lag < NZ:
-                stage(p - lag)
-        for action in extra.get(p, ()):
-            action()
-    own = ring(4, 0)
-    cp.arrived("py", pin, ypeer)
-    own = own + pin[...].astype(F32)
-    for n in range(3):
-        wq_sum[n] = own[:, n * 256 : (n + 1) * 256]
-    wo_sum[...] = own[:, 768:1024]
+    for name, *where in REDUCE:
+        actions[name](*where)
+    small_t_recv()
+    for n in range(NT):
+        cols = slice(n * SLICE, (n + 1) * SLICE)
+        act_out[:, cols] = small_out[n, 0:8]
+        gain_out[:, cols] = small_out[n, 8:9]
     for p in range(NZ):
         back_last(p)
 
@@ -559,27 +632,15 @@
 
 
 def on_device(inputs, upstream, action_ids, frame_time, action_table, gain, w_qkv, w_out):
-    f = lax.axis_index("frame")
-    actions = action_table.shape[0]
-    flat_ids = action_ids.reshape(4)
-    onehot = (flat_ids[:, None] == jnp.arange(actions, dtype=jnp.int32)).astype(F32)
-    embedded = jnp.einsum("fa,ad->fd", onehot, action_table, precision=lax.Precision.HIGHEST)
-    ids = jnp.broadcast_to(flat_ids.astype(F32)[:, None], (4, 128))
-
-    times = lax.dynamic_index_in_dim(frame_time, f // 4, 0, keepdims=False).reshape(NZ, 2)
-    times = times[(f - jnp.array(ORDER, jnp.int32)) % NZ]
-    code = times[:, :, None] + 64 * jnp.arange(SITES, dtype=jnp.int32)[None, None, :]
-    code = code.reshape(TOKENS).astype(F32)
-    code_col = jnp.broadcast_to(code[:, None], (TOKENS, 128))
-    code_row = jnp.broadcast_to(code[None, :], (8, TOKENS))
-
     vmem = pl.BlockSpec(memory_space=pltpu.VMEM)
     hbm = pl.BlockSpec(memory_space=pl.ANY)
+    smem = pl.BlockSpec(memory_space=pltpu.SMEM)
     chunk = (ROWS, SLICE)
     ring_shape = (4, 2, 64, 1024)
     scratch = [
         ((4, 144, WIDTH), BF16),
         ((4, 144, SLICE), BF16),
+        ((4, WIDTH), F32),
         ((NZ, 2) + chunk, BF16),
         ((NZ, 8, 128), F32),
         ((NZ, 8, 128), F32),
@@ -615,6 +676,10 @@
         ((64, 1024), BF16),
         ((64, 1024), BF16),
         ((2, NX, NZ) + chunk, BF16),
+        ((NZ, NX) + chunk, BF16),
+        ((NZ, 3) + chunk, BF16),
+        ((NZ, 3) + chunk, BF16),
+        ((NT, 16, SLICE), F32),
         ((8, SLICE), F32),
         ((8, SLICE), F32),
         ((16, SLICE), F32),
@@ -623,16 +688,17 @@
         ((4, 16, SLICE), F32),
         ((16, SLICE), F32),
     ]
-    grad_inputs, wq_sum, wo_sum, sums = pl.pallas_call(
+    grad_inputs, wq_sum, wo_sum, grad_gain, grad_actions = pl.pallas_call(
         kernel,
         out_shape=(
             jax.ShapeDtypeStruct((4, 144, WIDTH), BF16),
             jax.ShapeDtypeStruct((3, 64, 256), F32),
             jax.ShapeDtypeStruct((64, 256), F32),
-            jax.ShapeDtypeStruct((NT, 16, SLICE), F32),
+            jax.ShapeDtypeStruct((1, WIDTH), F32),
+            jax.ShapeDtypeStruct((8, WIDTH), F32),
         ),
-        in_specs=[hbm] * 4 + [vmem] * 5,
-        out_specs=(vmem,) * 4,
+        in_specs=[hbm] * 4 + [smem] * 2 + [vmem] * 2,
+        out_specs=(vmem,) * 5,
         scratch_shapes=[pltpu.VMEM(shape, kind) for shape, kind in scratch]
         + [
             pltpu.SemaphoreType.DMA((SLOTS,)),
@@ -647,19 +713,17 @@
         upstream.reshape(4, 144, WIDTH),
         w_qkv.transpose(1, 0, 2),
         w_out,
-        embedded,
-        ids,
+        action_ids.reshape(4),
+        frame_time,
+        action_table,
         gain.reshape(1, WIDTH),
-        code_col,
-        code_row,
     )
-    sums = sums.transpose(1, 0, 2).reshape(16, WIDTH)
     return (
         grad_inputs.reshape(inputs.shape),
         wq_sum.transpose(1, 0, 2),
         wo_sum,
-        sums[8],
-        sums[:8],
+        grad_gain.reshape(WIDTH),
+        grad_actions,
     )
 
 

time: 160 us -> 129 us (0.81)
  Pallas kernels: 145 us -> 121 us
  local copies, waits for them, and re-layouts: 11.9 us -> 7.24 us
    pallas_call x1, Pallas kernels: 145 us -> 121 us  [on_device(): pl.pallas_call(kernel, out_shape=(jax.ShapeDtypeStruct((4, 144, WIDTH), B...]
    slice x2 -> x0, local copies, waits for them, and re-layouts: 2.92 us -> none  [the longest x1 1.47 us: on_device(): sums[:8]]
    broadcast_in_dim x3 -> x0, local copies, waits for them, and re-layouts: 2.11 us -> none  [the longest x1 0.85 us: on_device(): code_col = jnp.broadcast_to(code[:, None], (TOKENS, 128))]
    unnamed x9 -> x13, local copies, waits for them, and re-layouts: 4.72 us -> 5.97 us
where the time goes in v3:
time: 129 us; the launch traced here: 128 us
  Pallas kernels  121 us (94%)
  local copies, waits for them, and re-layouts  7.24 us (6%)
    pallas_call x1, Pallas kernels, on_device(): pl.pallas_call(kernel, out_shape=(jax.ShapeDtypeStruct((4, 144, WIDTH), B...  121 us
    unnamed x13, local copies, waits for them, and re-layouts  5.97 us

profile of v3, /device:TPU:1, one launch (start us, length us, event | category | flops | bytes accessed | tf_op | source)
XLA Modules:
  0.0 128.5 jit_solution(1773559631899940387)
XLA Ops:
  0.6 1.3 reshape.30.ids
  1.9 120.6 %shard_map.119 = (bf16[4,144,2048]{2,1,0:T(8,128)(2,1)}, f32[3,64,256]{2,1,0:T(8,128)}, f32[64,256]{1,0:T(8,128)}, f32[1,2048]{1,0:T(1,128)}, f32[8,2048]{1,0:T(8,128)}) custom-call(bf16[4,144,2048]{2,1,0:T(8,128)(2,1)} %bitcast.7, bf16[4,144,2048]{2,1,0:T(8,128)(2,1)} %bitcast.8, bf16[3,64,256]{2,1,0:T(8,128)(2,1)} %bitcast.11, bf16[64,256]{1,0:T(8,128)(2,1)} %wo.1, ...), custom_call_target="tpu_custom_call" | custom-call | tf_op jit(solution)/shard_map/pallas_call | solution.py:691
  122.5 0.0 copy-start
  122.5 0.0 copy-start.2
  122.5 0.0 copy-start.3
  122.5 0.0 copy-start.1
  122.5 3.4 %copy.18 = bf16[2,2,144,2048]{3,2,1,0:T(8,128)(2,1)} copy(bf16[2,2,144,2048]{3,2,1,0:T(8,128)(2,1)} %bitcast.9) | data formatting | bytes 4718592
  125.9 0.0 copy-done
  125.9 0.7 copy.19
  126.6 0.0 copy-done.2
  126.6 0.6 copy.20
  127.2 0.0 copy-done.3
  127.3 0.6 copy.21
  127.9 0.0 copy-done.1
  127.9 0.6 copy.22
Async XLA Ops:
  122.5 3.5 %copy-start = (f32[3,64,256]{2,1,0:T(8,128)S(1)}, f32[3,64,256]{2,1,0:T(8,128)}, u32[]{:S(2)}) copy-start(f32[3,64,256]{2,1,0:T(8,128)} %get-tuple-element.11) | copy-start | bytes 589828
  122.5 4.1 %copy-start.2 = (f32[64,256]{1,0:T(8,128)S(1)}, f32[64,256]{1,0:T(8,128)}, u32[]{:S(2)}) copy-start(f32[64,256]{1,0:T(8,128)} %get-tuple-element.22) | copy-start | bytes 196612
  122.5 4.8 %copy-start.3 = (f32[1,2048]{1,0:T(1,128)S(1)}, f32[1,2048]{1,0:T(1,128)}, u32[]{:S(2)}) copy-start(f32[1,2048]{1,0:T(1,128)} %get-tuple-element.13) | copy-start | bytes 24580
  122.5 5.3 %copy-start.1 = (f32[8,2048]{1,0:T(8,128)S(1)}, f32[8,2048]{1,0:T(8,128)}, u32[]{:S(2)}) copy-start(f32[8,2048]{1,0:T(8,128)} %get-tuple-element.24) | copy-start | bytes 196612

commit v4 on v3

--- a/solution.py
+++ b/solution.py
@@ -21,7 +21,7 @@
 WIDTH = 2048
 VMEM_BYTES = 58 * 1024 * 1024
 ORDER = (0, 1, 7, 2, 6, 3, 5, 4)
-SLOTS = 400
+RECEIVED, SENT = 144, 15
 ACROSS = (3, 4, 5, 6, 7)
 GATHER = (
     ("w", 0, 0), ("zsend",), ("t0a", 0), ("t1a", 0), ("t1b", 0), ("w", 0, 1), ("w", 1, 0), ("t1c", 0),
@@ -64,38 +64,28 @@
 class Copies:
     def __init__(self, send_sems, recv_sems):
         self.send_sems, self.recv_sems = send_sems, recv_sems
-        self.slots, self.started = {}, []
-
-    def slot(self, name):
-        return self.slots.setdefault(name, len(self.slots))
-
-    def send(self, name, src, dst, device):
-        slot = self.slot(name)
-        copy = pltpu.make_async_remote_copy(
+        self.names, self.groups = {}, {}
+
+    def copy(self, name, group, src, dst, device):
+        return pltpu.make_async_remote_copy(
             src_ref=src,
             dst_ref=dst,
-            send_sem=self.send_sems.at[slot],
-            recv_sem=self.recv_sems.at[slot],
+            send_sem=self.send_sems.at[self.groups.setdefault(group, len(self.groups))],
+            recv_sem=self.recv_sems.at[self.names.setdefault(name, len(self.names))],
             device_id=device,
             device_id_type=MESH,
         )
-        copy.start()
-        self.started.append(copy)
-
-    def arrived(self, name, dst, device):
-        slot = self.slot(name)
-        pltpu.make_async_remote_copy(
-            src_ref=dst,
-            dst_ref=dst,
-            send_sem=self.send_sems.at[slot],
-            recv_sem=self.recv_sems.at[slot],
-            device_id=device,
-            device_id_type=MESH,
-        ).wait_recv()
-
-    def drain(self):
-        for copy in self.started:
-            copy.wait_send()
+
+    def send(self, name, src, dst, device, group):
+        self.copy(name, group, src, dst, device).start()
+
+    def arrived(self, name, landed, device):
+        group = next(iter(self.groups))
+        self.copy(name, group, landed, landed, device).wait_recv()
+
+    def drain(self, group, sent, device):
+        name = next(iter(self.names))
+        self.copy(name, group, sent, sent, device).wait_send()
 
 
 def kernel(
@@ -171,7 +161,7 @@
     names = lax.broadcasted_iota(jnp.int32, (8, WIDTH), 0)
     for i in range(4):
         embedded[i : i + 1] = jnp.sum(
-            jnp.where(names == ids[i], table[...], 0.0), 0, keepdims=True
+            jnp.where(names == ids[i // 2, i % 2], table[...], 0.0), 0, keepdims=True
         )
     load_in.wait()
 
@@ -211,7 +201,7 @@
             ).astype(BF16)
             meta[b * 4 + r] = jnp.concatenate(
                 [to_row(chunk(inverses))]
-                + [jnp.full((1, 128), ids[2 * b + fr].astype(F32), F32) for fr in range(2)]
+                + [jnp.full((1, 128), ids[b, fr].astype(F32), F32) for fr in range(2)]
                 + [jnp.zeros((5, 128), F32)],
                 0,
             )
@@ -221,8 +211,8 @@
     def tokens_send():
         for p in range(1, NZ):
             j = target(p)
-            cp.send(("z", p), xu.at[j], tok.at[yh, x, f], {"frame": j})
-            cp.send(("meta", p), meta.at[j], meta_in.at[f], {"frame": j})
+            cp.send(("z", p), xu.at[j], tok.at[yh, x, f], {"frame": j}, "z")
+            cp.send("meta", meta.at[j], meta_in.at[f], {"frame": j}, "meta")
         local(xu.at[f], tok.at[yh, x, f], 0).wait()
         meta_in[f] = meta[f]
 
@@ -230,60 +220,46 @@
         j = source(p)
         if p > 0:
             cp.arrived(("z", p), tok.at[yh, x, j], other)
-            cp.arrived(("meta", p), meta_in.at[j], other)
         mine = tok.at[yh, x, j, 0]
-        cp.send(("t0y", p), mine, mine, other)
-        cp.send(("t0r", p), mine, mine, right)
-        cp.send(("t0l", p), mine, mine, left)
+        cp.send(("t0y", p), mine, mine, other, "t")
+        cp.send(("t0x", p), mine, mine, right, "t")
+        cp.send(("last", p // 2), mine, mine, left, "t")
 
     def normed_b(p):
         theirs = tok.at[1 - yh, x, source(p), 0]
         cp.arrived(("t0y", p), theirs, other)
-        cp.send(("t0or", p), theirs, theirs, right)
-        cp.send(("t0ol", p), theirs, theirs, left)
+        cp.send(("last", p // 2), theirs, theirs, right, "t")
+        cp.send(("t0x", p), theirs, theirs, left, "t")
 
     def normed_c(p):
         j = source(p)
+        cp.arrived(("t0x", p), tok.at[0, 0, 0], left)
         block = tok.at[yh, xl, j, 0]
-        cp.arrived(("t0r", p), block, left)
-        cp.send(("t0fr", p), block, block, right)
+        cp.send(("last", p // 2), block, block, right, "t")
         block = tok.at[1 - yh, xr, j, 0]
-        cp.arrived(("t0ol", p), block, right)
-        cp.send(("t0fl", p), block, block, left)
+        cp.send(("last", p // 2), block, block, left, "t")
 
     def upstream_a(p):
         mine = tok.at[yh, x, source(p), 1]
-        cp.send(("t1r", p), mine, mine, right)
-        cp.send(("t1l", p), mine, mine, left)
-        cp.send(("t1y", p), mine, mine, other)
-        cp.send(("t1o", p), mine, mine, opposite)
+        cp.send(("t1x", p), mine, mine, right, "t")
+        cp.send(("t1x", p), mine, mine, left, "t")
+        cp.send(("last", p // 2), mine, mine, other, "t")
+        cp.send(("t1o", p), mine, mine, opposite, "t")
 
     def upstream_b(p):
         j = source(p)
-        for name, at, device in ((("t1r", p), xl, left), (("t1l", p), xr, right)):
-            block = tok.at[yh, at, j, 1]
-            cp.arrived(name, block, device)
-            cp.send((name, "y"), block, block, other)
+        cp.arrived(("t1x", p), tok.at[0, 0, 0], left)
+        for column in (xl, xr):
+            block = tok.at[yh, column, j, 1]
+            cp.send(("last", p // 2), block, block, other, "t")
 
     def upstream_c(p):
         block = tok.at[yh, xo, source(p), 1]
         cp.arrived(("t1o", p), block, opposite)
-        cp.send(("t1oy", p), block, block, other)
-
-    def tokens_last(p):
-        j = source(p)
-        cp.arrived(("t0l", p), tok.at[yh, xr, j, 0], right)
-        cp.arrived(("t0or", p), tok.at[1 - yh, xl, j, 0], left)
-        cp.arrived(("t0fr", p), tok.at[yh, xo, j, 0], left)
-        cp.arrived(("t0fl", p), tok.at[1 - yh, xo, j, 0], right)
-        cp.arrived(("t1y", p), tok.at[1 - yh, x, j, 1], other)
-        cp.arrived((("t1r", p), "y"), tok.at[1 - yh, xl, j, 1], other)
-        cp.arrived((("t1l", p), "y"), tok.at[1 - yh, xr, j, 1], other)
-        cp.arrived(("t1oy", p), tok.at[1 - yh, xo, j, 1], other)
+        cp.send(("last", p // 2), block, block, other, "t")
 
     def repack(pair):
-        for p in (2 * pair, 2 * pair + 1):
-            tokens_last(p)
+        cp.arrived(("last", pair), tok.at[:, :, 0:1], other)
         rows = slice(pair * 2 * ROWS, (pair + 1) * 2 * ROWS)
         for n in range(NT):
             cols = slice(n * SLICE, (n + 1) * SLICE)
@@ -303,36 +279,30 @@
             if o == 0:
                 for copy in load_w:
                     copy.wait()
-                cp.send("wy", block, block, ypeer)
+                cp.send("wy", block, block, ypeer, "w")
             else:
                 cp.arrived("wy", block, ypeer)
-            cp.send(("wu", 0, o), block, block, z_up)
-            cp.send(("wd", 0, o), block, block, z_down)
-            cp.send(("wc", 0, o), block, block, cpeer)
+            cp.send(("wu", 0, o), block, block, z_up, "w")
+            cp.send(("wd", 0, o), block, block, z_down, "w")
+            cp.send("wc", block, block, cpeer, "w")
         elif step < 4:
             block = w_rows(mod(f - step, NZ), row, c)
             cp.arrived(("wu", step - 1, o), block, z_down)
             if step < 3 or o == 0:
-                cp.send(("wu", step, o), block, block, z_up)
-            cp.send(("wc", step, o), block, block, cpeer)
+                cp.send(("wu", step, o), block, block, z_up, "w")
+            cp.send("wc", block, block, cpeer, "w")
             block = w_rows(mod(f + step, NZ), row, c)
             cp.arrived(("wd", step - 1, o), block, z_up)
             if step < 3 or o == 1:
-                cp.send(("wd", step, o), block, block, z_down)
-            cp.send(("wc", -step, o), block, block, cpeer)
+                cp.send(("wd", step, o), block, block, z_down, "w")
+            cp.send("wc", block, block, cpeer, "w")
         else:
             block = w_rows(mod(f + 4, NZ), row, c)
             if o == 0:
                 cp.arrived(("wu", 3, o), block, z_down)
             else:
                 cp.arrived(("wd", 3, o), block, z_up)
-            cp.send(("wc", 4, o), block, block, cpeer)
-
-    def weights_last():
-        for step in range(-3, 5):
-            for o in range(2):
-                row = yl if o == 0 else 1 - yl
-                cp.arrived(("wc", step, o), w_rows(mod(f - step, NZ), row, 1 - c), cpeer)
+            cp.send("wc", block, block, cpeer, "w")
 
     actions = {
         "w": weights, "zsend": tokens_send, "t0a": normed_a, "t0b": normed_b, "t0c": normed_c,
@@ -341,7 +311,7 @@
     for name, *where in GATHER:
         actions[name](*where)
     repack(3)
-    weights_last()
+    cp.arrived("wc", wts.at[0:1024], cpeer)
 
     @pl.loop(0, 3)
     def _(n):
@@ -382,14 +352,14 @@
 
     def send_across():
         for p in ACROSS:
-            cp.send(("ry", p), gn.at[1 - yh, :, target(p)], ry.at[p], other)
+            cp.send(("ry", p), gn.at[1 - yh, :, target(p)], ry.at[p], other, "ry")
 
     def reduce_a(p):
         j = target(p)
-        cp.send(("a", p), gn.at[1 - yh, xo, j], part_l.at[p], right)
-        cp.send(("b", p), gn.at[yh, xo, j], part_r.at[p], left)
-        cp.send(("c", p), gn.at[yh, xr, j], in_l.at[p, 0], right)
-        cp.send(("d", p), gn.at[1 - yh, xl, j], in_r.at[p, 1], left)
+        cp.send(("a", p), gn.at[1 - yh, xo, j], part_l.at[p], right, "r")
+        cp.send(("b", p), gn.at[yh, xo, j], part_r.at[p], left, "r")
+        cp.send(("in", p), gn.at[yh, xr, j], in_l.at[p, 0], right, "r")
+        cp.send(("in", p), gn.at[1 - yh, xl, j], in_r.at[p, 1], left, "r")
 
     def reduce_x(p):
         j = target(p)
@@ -399,14 +369,14 @@
                 rsend[p, i] = (
                     gn[yh, column, j].astype(F32) + ry[p, column].astype(F32)
                 ).astype(BF16)
-                cp.send(("rx", p, i), rsend.at[p, i], rin.at[p, i], device)
+                cp.send(("rx", p), rsend.at[p, i], rin.at[p, i], device, "rx")
             return
         cp.arrived(("a", p), part_l.at[p], left)
         sum_r[p] = (gn[1 - yh, xr, j].astype(F32) + part_l[p].astype(F32)).astype(BF16)
-        cp.send(("e", p), sum_r.at[p], in_l.at[p, 1], right)
+        cp.send(("in", p), sum_r.at[p], in_l.at[p, 1], right, "r")
         cp.arrived(("b", p), part_r.at[p], right)
         sum_l[p] = (gn[yh, xl, j].astype(F32) + part_r[p].astype(F32)).astype(BF16)
-        cp.send(("f", p), sum_l.at[p], in_r.at[p, 0], left)
+        cp.send(("in", p), sum_l.at[p], in_r.at[p, 0], left, "r")
 
     def send_means():
         product = jnp.zeros((TOKENS, 128), F32)
@@ -418,11 +388,11 @@
             m_part[pl.ds(source(p), 1), :] = to_row(column[p * ROWS : (p + 1) * ROWS])
         m_in[t] = m_part[...]
         for k, peer in enumerate(tensors):
-            cp.send(("m", k), m_part, m_in.at[t], peer)
+            cp.send("m", m_part, m_in.at[t], peer, "m")
 
     def take_means():
-        for k, peer in enumerate(tensors):
-            cp.arrived(("m", k), m_in.at[mod(t - k - 1, NT)], peer)
+        cp.arrived("meta", meta_in.at[0:7], other)
+        cp.arrived("m", m_in.at[0:7], other)
         row_sum = m_in[0]
         for k in range(1, NT):
             row_sum = row_sum + m_in[k]
@@ -441,7 +411,7 @@
         for r in range(4):
             gw[n, r // 2, r % 2, :, 0:768] = term[64 * r : 64 * r + 64]
             gw[n, r // 2, r % 2, :, 768:1024] = term_out[64 * r : 64 * r + 64]
-        cp.send(("core", i), gw.at[n, :, 1 - c], cin.at[n], cpeer)
+        cp.send(("core", i), gw.at[n, :, 1 - c], cin.at[n], cpeer, "core")
 
     def partner_terms(*which):
         for i in which:
@@ -451,15 +421,12 @@
 
     def sum_y(p):
         j = target(p)
-        cp.arrived(("c", p), in_l.at[p, 0], left)
-        cp.arrived(("d", p), in_r.at[p, 1], right)
-        cp.arrived(("e", p), in_l.at[p, 1], left)
-        cp.arrived(("f", p), in_r.at[p, 0], right)
+        cp.arrived(("in", p), ry.at[0], left)
         theirs = (
             gn[1 - yh, x, j].astype(F32) + in_l[p, 1].astype(F32) + in_r[p, 1].astype(F32)
         )
         ysend[p] = theirs.astype(BF16)
-        cp.send(("sy", p), ysend.at[p], yin.at[p], other)
+        cp.send(("sy", p), ysend.at[p], yin.at[p], other, "r")
 
     def to_frames(p):
         j = target(p)
@@ -468,8 +435,8 @@
             take_means()
         grad_norm = gn[yh, x, j].astype(F32)
         if p in ACROSS:
-            for i, device in enumerate((left, right, opposite)):
-                cp.arrived(("rx", p, i), rin.at[p, i], device)
+            cp.arrived(("rx", p), rin.at[p], left)
+            for i in range(3):
                 grad_norm = grad_norm + rin[p, i].astype(F32)
             grad_norm = grad_norm + ry[p, x].astype(F32)
         else:
@@ -490,7 +457,7 @@
         if p == 0:
             local(zsend.at[0], full.at[yh, x, f], 0).wait()
         else:
-            cp.send(("bz", p), zsend.at[p], full.at[yh, x, f], {"frame": j})
+            cp.send(("bz", p), zsend.at[p], full.at[yh, x, f], {"frame": j}, "bz")
         gterm[0:1] += jnp.sum(grad_norm * rows, 0, keepdims=True)
         labels = lax.broadcasted_iota(jnp.int32, (8, SLICE), 0).astype(F32)
         for fr in range(2):
@@ -503,32 +470,24 @@
         mine = full.at[yh, x, j]
         if p > 0:
             cp.arrived(("bz", p), mine, other)
-        cp.send(("by", p), mine, mine, other)
-        cp.send(("br", p), mine, mine, right)
-        cp.send(("bl", p), mine, mine, left)
+        cp.send(("by", p), mine, mine, other, "b")
+        cp.send(("bx", p), mine, mine, right, "b")
+        cp.send("back", mine, mine, left, "b")
 
     def back_x(p):
         j = source(p)
         theirs = full.at[1 - yh, x, j]
         cp.arrived(("by", p), theirs, other)
-        cp.send(("bor", p), theirs, theirs, right)
-        cp.send(("bol", p), theirs, theirs, left)
+        cp.send("back", theirs, theirs, right, "b")
+        cp.send(("bx", p), theirs, theirs, left, "b")
 
     def back_forward(p):
         j = source(p)
+        cp.arrived(("bx", p), full.at[0, 0, 0:2], left)
         block = full.at[yh, xl, j]
-        cp.arrived(("br", p), block, left)
-        cp.send(("bfr", p), block, block, right)
+        cp.send("back", block, block, right, "b")
         block = full.at[1 - yh, xr, j]
-        cp.arrived(("bol", p), block, right)
-        cp.send(("bfl", p), block, block, left)
-
-    def back_last(p):
-        j = source(p)
-        cp.arrived(("bl", p), full.at[yh, xr, j], right)
-        cp.arrived(("bor", p), full.at[1 - yh, xl, j], left)
-        cp.arrived(("bfr", p), full.at[yh, xo, j], left)
-        cp.arrived(("bfl", p), full.at[1 - yh, xo, j], right)
+        cp.send("back", block, block, left, "b")
 
     def term(j, o):
         row = yl if o == 0 else 1 - yl
@@ -539,9 +498,9 @@
             partner_terms(0)
             far = blocks[0]
             rs_up[0, 0] = term(far, 0).astype(BF16)
-            cp.send(("ru", 0, 0), rs_up.at[0, 0], ri_up.at[0, 0], z_up)
+            cp.send(("ru", 0, 0), rs_up.at[0, 0], ri_up.at[0, 0], z_up, "ring")
             rs_down[0, 1] = term(far, 1).astype(BF16)
-            cp.send(("rd", 0, 1), rs_down.at[0, 1], ri_down.at[0, 1], z_down)
+            cp.send(("rd", 0, 1), rs_down.at[0, 1], ri_down.at[0, 1], z_down, "ring")
         elif step < 4:
             partner_terms(2 * step - 1, 2 * step)
             value = term(blocks[2 * step - 1], o)
@@ -549,13 +508,13 @@
                 cp.arrived(("ru", step - 1, o), ri_up.at[step - 1, o], z_down)
                 value = value + ri_up[step - 1, o].astype(F32)
             rs_up[step, o] = value.astype(BF16)
-            cp.send(("ru", step, o), rs_up.at[step, o], ri_up.at[step, o], z_up)
+            cp.send(("ru", step, o), rs_up.at[step, o], ri_up.at[step, o], z_up, "ring")
             value = term(blocks[2 * step], o)
             if step > 1 or o == 1:
                 cp.arrived(("rd", step - 1, o), ri_down.at[step - 1, o], z_up)
                 value = value + ri_down[step - 1, o].astype(F32)
             rs_down[step, o] = value.astype(BF16)
-            cp.send(("rd", step, o), rs_down.at[step, o], ri_down.at[step, o], z_down)
+            cp.send(("rd", step, o), rs_down.at[step, o], ri_down.at[step, o], z_down, "ring")
         else:
             partner_terms(7)
             cp.arrived(("ru", 3, o), ri_up.at[3, o], z_down)
@@ -563,7 +522,7 @@
             value = term(f, o) + ri_up[3, o].astype(F32) + ri_down[3, o].astype(F32)
             if o == 1:
                 psend[...] = value.astype(BF16)
-                cp.send("py", psend, pin, ypeer)
+                cp.send("py", psend, pin, ypeer, "ring")
                 return
             cp.arrived("py", pin, ypeer)
             value = value + pin[...].astype(F32)
@@ -576,33 +535,30 @@
         small[8:16] = gterm[...] * gain_inv
         zin[f] = small[...]
         for k, peer in enumerate(frames):
-            cp.send(("sz", k), small, zin.at[f], peer)
+            cp.send("sz", small, zin.at[f], peer, "sz")
 
     def small_z_recv():
-        for k, peer in enumerate(frames):
-            cp.arrived(("sz", k), zin.at[mod(f - k - 1, NZ)], peer)
+        cp.arrived("sz", zin.at[0:7], other)
         acc = zin[0]
         for k in range(1, NZ):
             acc = acc + zin[k]
         sent[...] = acc
         sin[s] = acc
         for k, peer in enumerate(spaces):
-            cp.send(("ss", k), sent, sin.at[s], peer)
+            cp.send("ss", sent, sin.at[s], peer, "ss")
 
     def small_s_recv():
-        for k, peer in enumerate(spaces):
-            cp.arrived(("ss", k), sin.at[mod(s - k - 1, 4)], peer)
+        cp.arrived("ss", sin.at[0:3], other)
         acc = sin[0]
         for k in range(1, 4):
             acc = acc + sin[k]
         total[...] = acc
         small_out[t] = acc
         for k, peer in enumerate(tensors):
-            cp.send(("st", k), total, small_out.at[t], peer)
+            cp.send("st", total, small_out.at[t], peer, "st")
 
     def small_t_recv():
-        for k, peer in enumerate(tensors):
-            cp.arrived(("st", k), small_out.at[mod(t - k - 1, NT)], peer)
+        cp.arrived("st", small_out.at[0:7], other)
 
     actions = {
         "np": norm_parts, "np0s": send_across, "ra": reduce_a, "rx": reduce_x, "m": send_means,
@@ -616,8 +572,7 @@
         cols = slice(n * SLICE, (n + 1) * SLICE)
         act_out[:, cols] = small_out[n, 0:8]
         gain_out[:, cols] = small_out[n, 8:9]
-    for p in range(NZ):
-        back_last(p)
+    cp.arrived("back", full.at[:, :, 0:4], other)
 
     for n in range(NT):
         cols = slice(n * SLICE, (n + 1) * SLICE)
@@ -628,7 +583,35 @@
                 out[2 * b + fr, :, cols] = jnp.concatenate(
                     [block[rows] for block in blocks], 0
                 ).astype(BF16)
-    cp.drain()
+    first = len(ACROSS)
+    sent = {
+        "w": wts.at[0:1984], "z": xu.at[0:7], "meta": meta.at[0:7], "t": tok.at[:, :, 0:7],
+        "r": rin.at[0:7], "rx": rin.at[0:first], "ry": ry.at[0:first],
+        "bz": zsend.at[0:7], "b": full.at[:, :, 0:7], "core": cin, "ring": wts.at[0:960],
+        "m": m_in.at[0:7], "sz": zin.at[0:7], "ss": sin.at[0:3], "st": small_out.at[0:7],
+    }
+    for group in cp.groups:
+        cp.drain(group, sent[group], other)
+
+
+def finish_kernel(*refs):
+    arrays, outs, held, sems = refs[:5], refs[5:10], refs[10:15], refs[15]
+    parts = [(n, (slice(None),)) for n in range(1, 5)] + [(0, (n,)) for n in range(4)]
+    taken = [
+        pltpu.make_async_copy(arrays[n].at[at], held[n].at[at], sems.at[0, i])
+        for i, (n, at) in enumerate(parts)
+    ]
+    given = [
+        pltpu.make_async_copy(held[n].at[at], outs[n].at[at], sems.at[1, i])
+        for i, (n, at) in enumerate(parts)
+    ]
+    for copy in taken:
+        copy.start()
+    for first, second in zip(taken, given):
+        first.wait()
+        second.start()
+    for copy in given:
+        copy.wait()
 
 
 def on_device(inputs, upstream, action_ids, frame_time, action_table, gain, w_qkv, w_out):
@@ -688,7 +671,7 @@
         ((4, 16, SLICE), F32),
         ((16, SLICE), F32),
     ]
-    grad_inputs, wq_sum, wo_sum, grad_gain, grad_actions = pl.pallas_call(
+    results = pl.pallas_call(
         kernel,
         out_shape=(
             jax.ShapeDtypeStruct((4, 144, WIDTH), BF16),
@@ -701,8 +684,8 @@
         out_specs=(vmem,) * 5,
         scratch_shapes=[pltpu.VMEM(shape, kind) for shape, kind in scratch]
         + [
-            pltpu.SemaphoreType.DMA((SLOTS,)),
-            pltpu.SemaphoreType.DMA((SLOTS,)),
+            pltpu.SemaphoreType.DMA((SENT,)),
+            pltpu.SemaphoreType.DMA((RECEIVED,)),
             pltpu.SemaphoreType.DMA((6,)),
         ],
         compiler_params=pltpu.CompilerParams(
@@ -713,11 +696,20 @@
         upstream.reshape(4, 144, WIDTH),
         w_qkv.transpose(1, 0, 2),
         w_out,
-        action_ids.reshape(4),
+        action_ids,
         frame_time,
         action_table,
         gain.reshape(1, WIDTH),
     )
+    grad_inputs, wq_sum, wo_sum, grad_gain, grad_actions = pl.pallas_call(
+        finish_kernel,
+        out_shape=tuple(jax.ShapeDtypeStruct(a.shape, a.dtype) for a in results),
+        in_specs=[hbm] * 5,
+        out_specs=(hbm,) * 5,
+        scratch_shapes=[pltpu.VMEM(a.shape, a.dtype) for a in results]
+        + [pltpu.SemaphoreType.DMA((2, 8))],
+        compiler_params=pltpu.CompilerParams(vmem_limit_bytes=VMEM_BYTES),
+    )(*results)
     return (
         grad_inputs.reshape(inputs.shape),
         wq_sum.transpose(1, 0, 2),

time: 129 us -> 118 us (0.915)
  local copies, waits for them, and re-layouts: 7.24 us -> 0 us
  Pallas kernels: 121 us -> 117 us
    pallas_call x1, Pallas kernels: 121 us -> 114 us  [on_device(): pl.pallas_call(kernel, out_shape=(jax.ShapeDtypeStruct((4, 144, WIDTH), B...]
    unnamed x13 -> x0, local copies, waits for them, and re-layouts: 5.97 us -> none
    pallas_call x0 -> x1, Pallas kernels: none -> 2.79 us  [on_device(): pl.pallas_call(finish_kernel, out_shape=tuple((jax.ShapeDtypeStruct(a.sha...]
where the time goes in v4:
time: 118 us; the launch traced here: 117 us
  Pallas kernels  117 us (99%)
    pallas_call x1, Pallas kernels, on_device(): pl.pallas_call(kernel, out_shape=(jax.ShapeDtypeStruct((4, 144, WIDTH), B...  114 us
    pallas_call x1, Pallas kernels, on_device(): pl.pallas_call(finish_kernel, out_shape=tuple((jax.ShapeDtypeStruct(a.sha...  2.79 us

profile of v4, /device:TPU:1, one launch (start us, length us, event | category | flops | bytes accessed | tf_op | source)
XLA Modules:
  0.0 117.4 jit_solution(10956352926254972751)
XLA Ops:
  0.6 113.8 %shard_map.119 = (bf16[4,144,2048]{2,1,0:T(8,128)(2,1)}, f32[3,64,256]{2,1,0:T(8,128)}, f32[64,256]{1,0:T(8,128)}, f32[1,2048]{1,0:T(1,128)}, f32[8,2048]{1,0:T(8,128)}) custom-call(bf16[4,144,2048]{2,1,0:T(8,128)(2,1)} %bitcast.7, bf16[4,144,2048]{2,1,0:T(8,128)(2,1)} %bitcast.8, bf16[3,64,256]{2,1,0:T(8,128)(2,1)} %bitcast.9, bf16[64,256]{1,0:T(8,128)(2,1)} %wo.1, ...), custom_call_target="tpu_custom_call" | custom-call | tf_op jit(solution)/shard_map/pallas_call | solution.py:674
  114.5 2.8 %shard_map.120 = (bf16[4,144,2048]{2,1,0:T(8,128)(2,1)}, f32[3,64,256]{2,1,0:T(8,128)}, f32[64,256]{1,0:T(8,128)}, f32[1,2048]{1,0:T(1,128)}, f32[8,2048]{1,0:T(8,128)}) custom-call(bf16[4,144,2048]{2,1,0:T(8,128)(2,1)} %get-tuple-element.15.refs_0_, f32[3,64,256]{2,1,0:T(8,128)} %get-tuple-element.16.refs_1_, f32[64,256]{1,0:T(8,128)} %get-tuple-element.17.refs_2_, ...), custom_call_target="tpu_custom_call" | custom-call | tf_op jit(solution)/shard_map/pallas_call | solution.py:704

commit v5 on v4

--- a/solution.py
+++ b/solution.py
@@ -22,26 +22,27 @@
 VMEM_BYTES = 58 * 1024 * 1024
 ORDER = (0, 1, 7, 2, 6, 3, 5, 4)
 RECEIVED, SENT = 144, 15
-ACROSS = (3, 4, 5, 6, 7)
+BACK = (0, 1, 7, 2, 6, 3, 5, 4)
+ACROSS = (1, 3, 5, 7)
 GATHER = (
-    ("w", 0, 0), ("zsend",), ("t0a", 0), ("t1a", 0), ("t1b", 0), ("w", 0, 1), ("w", 1, 0), ("t1c", 0),
-    ("t0b", 0), ("t0a", 1), ("t1a", 1), ("t0a", 2), ("t1a", 2), ("t0c", 0), ("t0b", 1), ("t0a", 3),
-    ("t1a", 3), ("t0a", 4), ("t1a", 4), ("t1b", 1), ("t1c", 1), ("t0b", 2), ("t1b", 2), ("t0b", 3),
-    ("t1c", 2), ("t0b", 4), ("t0a", 5), ("t1a", 5), ("t0a", 6), ("t1a", 6), ("t0c", 1), ("t1b", 3),
-    ("t1c", 3), ("t0a", 7), ("t1a", 7), ("t1b", 4), ("t1c", 4), ("w", 1, 1), ("t0c", 2), ("t0b", 5),
-    ("t0c", 3), ("t0c", 4), ("t0b", 6), ("w", 2, 0), ("t1b", 5), ("t1c", 5), ("t1b", 6), ("w", 2, 1),
-    ("t0b", 7), ("t1c", 6), ("rp", 0), ("w", 3, 0), ("t1b", 7), ("t1c", 7), ("t0c", 5), ("w", 3, 1),
-    ("rp", 1), ("t0c", 6), ("w", 4, 0), ("t0c", 7), ("rp", 2), ("w", 4, 1),
+    ("zsend",), ("w", 0, 0), ("t0a", 0), ("t1a", 0), ("t0a", 1), ("t1a", 1), ("t0a", 2), ("t1a", 2),
+    ("t1b", 0), ("t1c", 0), ("w", 0, 1), ("t0b", 0), ("t0a", 3), ("t1a", 3), ("t0a", 4), ("t1a", 4),
+    ("t1b", 1), ("t0b", 1), ("t1c", 1), ("t0b", 2), ("t1b", 2), ("t1c", 2), ("t0c", 0), ("t0a", 5),
+    ("t1a", 5), ("t0a", 6), ("t1a", 6), ("t1b", 3), ("t0b", 3), ("t1c", 3), ("t0b", 4), ("t0a", 7),
+    ("t1a", 7), ("t1b", 4), ("t1c", 4), ("t0c", 1), ("w", 1, 0), ("t0c", 2), ("t1b", 5), ("w", 1, 1),
+    ("t1c", 5), ("t0b", 5), ("t1b", 6), ("t0b", 6), ("t1c", 6), ("w", 2, 0), ("t0c", 3), ("t0c", 4),
+    ("w", 2, 1), ("t1b", 7), ("t0b", 7), ("t1c", 7), ("rp", 0), ("w", 3, 0), ("t0c", 5), ("t0c", 6),
+    ("rp", 1), ("w", 3, 1), ("t0c", 7), ("rp", 2), ("w", 4, 0), ("w", 4, 1),
 )
 REDUCE = (
-    ("np", 0), ("np0s",), ("np", 1), ("ra", 0), ("ra", 1), ("ra", 2), ("m",), ("wt", 0), ("wt", 1), ("wt", 2),
-    ("rx", 0), ("rx", 3), ("wt", 3), ("rg", 0), ("rx", 1), ("wt", 4), ("wt", 5), ("rx", 2), ("rx", 4),
-    ("wt", 6), ("sy", 0), ("wt", 7), ("tf", 3), ("rg", 1, 0), ("rg", 1, 1), ("rx", 5), ("sy", 1), ("sy", 2),
-    ("tf", 4), ("rx", 6), ("ba", 3), ("tf", 5), ("rx", 7), ("rg", 2, 0), ("tf", 0), ("ba", 0), ("tf", 6),
-    ("tf", 1), ("tf", 2), ("bb", 3), ("rg", 2, 1), ("ba", 4), ("tf", 7), ("bb", 0), ("s0",), ("ba", 5),
-    ("bc", 3), ("bb", 4), ("bc", 0), ("rg", 3, 0), ("bb", 5), ("ba", 6), ("ba", 1), ("ba", 2), ("bc", 4),
-    ("bc", 5), ("bb", 6), ("rg", 3, 1), ("bb", 1), ("bb", 2), ("ba", 7), ("s1",), ("bc", 6), ("bb", 7),
-    ("s2",), ("bc", 1), ("bc", 2), ("rg", 4, 1), ("bc", 7), ("rg", 4, 0),
+    ("np", 0), ("np0s",), ("wt", 0), ("np", 1), ("ra", 0), ("ra", 2), ("ra", 4), ("ra", 6), ("wt", 1),
+    ("wt", 2), ("wt", 3), ("rg", 0), ("wt", 4), ("wt", 5), ("rx", 0), ("wt", 6), ("rx", 1), ("wt", 7), ("m",),
+    ("rx", 2), ("rx", 4), ("rx", 3), ("rg", 1, 0), ("rg", 1, 1), ("rx", 6), ("sy", 0), ("rx", 5), ("tf", 1),
+    ("sy", 2), ("rg", 2, 0), ("sy", 4), ("rx", 7), ("tf", 0), ("ba", 0), ("tf", 3), ("tf", 2), ("rg", 2, 1),
+    ("sy", 6), ("tf", 4), ("ba", 1), ("tf", 5), ("bb", 0), ("tf", 7), ("tf", 6), ("rg", 3, 0), ("bb", 1),
+    ("ba", 2), ("s0",), ("bc", 0), ("ba", 3), ("bc", 1), ("bb", 2), ("rg", 3, 1), ("ba", 4), ("bb", 3),
+    ("bc", 2), ("ba", 5), ("bb", 4), ("bc", 3), ("ba", 6), ("ba", 7), ("bb", 5), ("s1",), ("bc", 4),
+    ("bb", 6), ("bb", 7), ("rg", 4, 1), ("s2",), ("bc", 5), ("bc", 6), ("bc", 7), ("rg", 4, 0),
 )
 
 
@@ -310,15 +311,19 @@
     }
     for name, *where in GATHER:
         actions[name](*where)
+    cp.arrived("wc", wts.at[0:1024], cpeer)
+
+    def project(rows):
+        @pl.loop(0, 3)
+        def _(n):
+            at = pl.ds(pl.multiple_of(n * 256, 256), 256)
+            qkv[rows, at] = nn(normed[rows], wts[:, at]).astype(BF16)
+
+        qkv[rows, 768:1024] = nn(up[rows], wts[:, 768:1024]).astype(BF16)
+
+    project(slice(0, 6 * ROWS))
     repack(3)
-    cp.arrived("wc", wts.at[0:1024], cpeer)
-
-    @pl.loop(0, 3)
-    def _(n):
-        at = pl.ds(pl.multiple_of(n * 256, 256), 256)
-        qkv[:, at] = nn(normed[...], wts[:, at]).astype(BF16)
-
-    qkv[:, 768:1024] = nn(up[...], wts[:, 768:1024]).astype(BF16)
+    project(slice(6 * ROWS, TOKENS))
 
     scale = 1.0 / math.sqrt(HEAD)
     half = TOKENS // 2
@@ -345,6 +350,12 @@
         for p in range(NZ):
             gn[plane, column, source(p)] = term[p * ROWS : (p + 1) * ROWS].astype(BF16)
 
+    def back_source(p):
+        return mod(f - BACK[p], NZ)
+
+    def back_target(p):
+        return mod(f + BACK[p], NZ)
+
     def norm_parts(which):
         plane = 1 - yh if which == 0 else yh
         for column in range(NX):
@@ -352,17 +363,17 @@
 
     def send_across():
         for p in ACROSS:
-            cp.send(("ry", p), gn.at[1 - yh, :, target(p)], ry.at[p], other, "ry")
+            cp.send(("ry", p), gn.at[1 - yh, :, back_target(p)], ry.at[p], other, "ry")
 
     def reduce_a(p):
-        j = target(p)
+        j = back_target(p)
         cp.send(("a", p), gn.at[1 - yh, xo, j], part_l.at[p], right, "r")
         cp.send(("b", p), gn.at[yh, xo, j], part_r.at[p], left, "r")
         cp.send(("in", p), gn.at[yh, xr, j], in_l.at[p, 0], right, "r")
         cp.send(("in", p), gn.at[1 - yh, xl, j], in_r.at[p, 1], left, "r")
 
     def reduce_x(p):
-        j = target(p)
+        j = back_target(p)
         if p in ACROSS:
             cp.arrived(("ry", p), ry.at[p], other)
             for i, (column, device) in enumerate(((xr, right), (xl, left), (xo, opposite))):
@@ -420,7 +431,7 @@
                 cp.arrived(("core", i), cin.at[blocks[i]], cpeer)
 
     def sum_y(p):
-        j = target(p)
+        j = back_target(p)
         cp.arrived(("in", p), ry.at[0], left)
         theirs = (
             gn[1 - yh, x, j].astype(F32) + in_l[p, 1].astype(F32) + in_r[p, 1].astype(F32)
@@ -429,7 +440,7 @@
         cp.send(("sy", p), ysend.at[p], yin.at[p], other, "r")
 
     def to_frames(p):
-        j = target(p)
+        j = back_target(p)
         if not shared.issuperset(("mean",)):
             shared.add("mean")
             take_means()
@@ -454,8 +465,8 @@
             gain_t * grad_norm - rows * (gain_inv * mean)
         )
         zsend[p] = grad_hidden.astype(BF16)
-        if p == 0:
-            local(zsend.at[0], full.at[yh, x, f], 0).wait()
+        if BACK[p] == 0:
+            local(zsend.at[p], full.at[yh, x, f], 0).wait()
         else:
             cp.send(("bz", p), zsend.at[p], full.at[yh, x, f], {"frame": j}, "bz")
         gterm[0:1] += jnp.sum(grad_norm * rows, 0, keepdims=True)
@@ -466,23 +477,23 @@
             act[...] += jnp.where(labels == name, frame_sum, 0.0)
 
     def back_y(p):
-        j = source(p)
+        j = back_source(p)
         mine = full.at[yh, x, j]
-        if p > 0:
+        if BACK[p] > 0:
             cp.arrived(("bz", p), mine, other)
         cp.send(("by", p), mine, mine, other, "b")
         cp.send(("bx", p), mine, mine, right, "b")
         cp.send("back", mine, mine, left, "b")
 
     def back_x(p):
-        j = source(p)
+        j = back_source(p)
         theirs = full.at[1 - yh, x, j]
         cp.arrived(("by", p), theirs, other)
         cp.send("back", theirs, theirs, right, "b")
         cp.send(("bx", p), theirs, theirs, left, "b")
 
     def back_forward(p):
-        j = source(p)
+        j = back_source(p)
         cp.arrived(("bx", p), full.at[0, 0, 0:2], left)
         block = full.at[yh, xl, j]
         cp.send("back", block, block, right, "b")
@@ -586,7 +597,7 @@
     first = len(ACROSS)
     sent = {
         "w": wts.at[0:1984], "z": xu.at[0:7], "meta": meta.at[0:7], "t": tok.at[:, :, 0:7],
-        "r": rin.at[0:7], "rx": rin.at[0:first], "ry": ry.at[0:first],
+        "r": {3: rin.at[0:7], 4: ry.at[0:7], 6: full.at[:, 0:3, 0:7]}.get(NZ - first), "rx": rin.at[0:first], "ry": ry.at[0:first],
         "bz": zsend.at[0:7], "b": full.at[:, :, 0:7], "core": cin, "ring": wts.at[0:960],
         "m": m_in.at[0:7], "sz": zin.at[0:7], "ss": sin.at[0:3], "st": small_out.at[0:7],
     }

time: 118 us -> 111 us (0.941)
  Pallas kernels: 117 us -> 110 us
    pallas_call x1, Pallas kernels: 114 us -> 107 us  [on_device(): pl.pallas_call(kernel, out_shape=(jax.ShapeDtypeStruct((4, 144, WIDTH), B...]
where the time goes in v5:
time: 111 us
  Pallas kernels  110 us (99%)
    pallas_call x1, Pallas kernels, on_device(): pl.pallas_call(kernel, out_shape=(jax.ShapeDtypeStruct((4, 144, WIDTH), B...  107 us
    pallas_call x1, Pallas kernels, on_device(): pl.pallas_call(finish_kernel, out_shape=tuple((jax.ShapeDtypeStruct(a.sha...  2.79 us

profile of v5, /device:TPU:1, one launch (start us, length us, event | category | flops | bytes accessed | tf_op | source)
XLA Modules:
  0.0 110.8 jit_solution(17916223800740015897)
XLA Ops:
  0.6 107.3 %shard_map.119 = (bf16[4,144,2048]{2,1,0:T(8,128)(2,1)}, f32[3,64,256]{2,1,0:T(8,128)}, f32[64,256]{1,0:T(8,128)}, f32[1,2048]{1,0:T(1,128)}, f32[8,2048]{1,0:T(8,128)}) custom-call(bf16[4,144,2048]{2,1,0:T(8,128)(2,1)} %bitcast.7, bf16[4,144,2048]{2,1,0:T(8,128)(2,1)} %bitcast.8, bf16[3,64,256]{2,1,0:T(8,128)(2,1)} %bitcast.9, bf16[64,256]{1,0:T(8,128)(2,1)} %wo.1, ...), custom_call_target="tpu_custom_call" | custom-call | tf_op jit(solution)/shard_map/pallas_call | solution.py:685
  108.0 2.8 %shard_map.120 = (bf16[4,144,2048]{2,1,0:T(8,128)(2,1)}, f32[3,64,256]{2,1,0:T(8,128)}, f32[64,256]{1,0:T(8,128)}, f32[1,2048]{1,0:T(1,128)}, f32[8,2048]{1,0:T(8,128)}) custom-call(bf16[4,144,2048]{2,1,0:T(8,128)(2,1)} %get-tuple-element.15.refs_0_, f32[3,64,256]{2,1,0:T(8,128)} %get-tuple-element.16.refs_1_, f32[64,256]{1,0:T(8,128)} %get-tuple-element.17.refs_2_, ...), custom_call_target="tpu_custom_call" | custom-call | tf_op jit(solution)/shard_map/pallas_call | solution.py:715

commit v6 on v5

--- a/solution.py
+++ b/solution.py
@@ -92,7 +92,7 @@
 def kernel(
     inputs, upstream, w3, wo, ids, times, table, gain,
     out, wq_sum, wo_sum, gain_out, act_out,
-    in_v, up_v, embedded, xu, meta, meta_in, tok, wts, normed, up, bias, qkv, mixed, grads, probs, dscore,
+    in_v, up_v, embedded, out_v, xu, meta, meta_in, tok, wts, normed, up, bias, qkv, mixed, grads, probs, dscore,
     m_part, m_in, m_sum, gn, gw, part_l, part_r, sum_l, sum_r, in_l, in_r, ysend, yin, zsend,
     cin, rs_up, rs_down, ri_up, ri_down, psend, pin, full, ry, rsend, rin, small_out,
     act, gterm, small, zin, sent, sin, total,
@@ -585,15 +585,18 @@
         gain_out[:, cols] = small_out[n, 8:9]
     cp.arrived("back", full.at[:, :, 0:4], other)
 
-    for n in range(NT):
-        cols = slice(n * SLICE, (n + 1) * SLICE)
-        for b in range(2):
+    written = []
+    for b in range(2):
+        for n in range(NT):
+            cols = slice(n * SLICE, (n + 1) * SLICE)
             blocks = [full[n // NX, n % NX, b * 4 + r].astype(F32) for r in range(4)]
             for fr in range(2):
                 rows = slice(fr * SITES, (fr + 1) * SITES)
-                out[2 * b + fr, :, cols] = jnp.concatenate(
+                out_v[2 * b + fr, :, cols] = jnp.concatenate(
                     [block[rows] for block in blocks], 0
                 ).astype(BF16)
+        for fr in range(2):
+            written.append(local(out_v.at[2 * b + fr], out.at[2 * b + fr], 2 * b + fr))
     first = len(ACROSS)
     sent = {
         "w": wts.at[0:1984], "z": xu.at[0:7], "meta": meta.at[0:7], "t": tok.at[:, :, 0:7],
@@ -603,6 +606,8 @@
     }
     for group in cp.groups:
         cp.drain(group, sent[group], other)
+    for copy in written:
+        copy.wait()
 
 
 def finish_kernel(*refs):
@@ -635,6 +640,7 @@
         ((4, 144, WIDTH), BF16),
         ((4, 144, SLICE), BF16),
         ((4, WIDTH), F32),
+        ((4, 144, WIDTH), BF16),
         ((NZ, 2) + chunk, BF16),
         ((NZ, 8, 128), F32),
         ((NZ, 8, 128), F32),
@@ -692,7 +698,7 @@
             jax.ShapeDtypeStruct((8, WIDTH), F32),
         ),
         in_specs=[hbm] * 4 + [smem] * 2 + [vmem] * 2,
-        out_specs=(vmem,) * 5,
+        out_specs=(hbm,) + (vmem,) * 4,
         scratch_shapes=[pltpu.VMEM(shape, kind) for shape, kind in scratch]
         + [
             pltpu.SemaphoreType.DMA((SENT,)),

time: 111 us -> 111 us (level)
  no operation moved by 1% of the time
where the time goes in v6:
time: 111 us
  Pallas kernels  111 us (100%)
    pallas_call x1, Pallas kernels, on_device(): pl.pallas_call(kernel, out_shape=(jax.ShapeDtypeStruct((4, 144, WIDTH), B...  108 us
    pallas_call x1, Pallas kernels, on_device(): pl.pallas_call(finish_kernel, out_shape=tuple((jax.ShapeDtypeStruct(a.sha...  2.79 us

profile of v6, /device:TPU:1, one launch (start us, length us, event | category | flops | bytes accessed | tf_op | source)
XLA Modules:
  0.0 111.2 jit_solution(10730873232855770923)
XLA Ops:
  0.6 107.8 %shard_map.119 = (bf16[4,144,2048]{2,1,0:T(8,128)(2,1)}, f32[3,64,256]{2,1,0:T(8,128)}, f32[64,256]{1,0:T(8,128)}, f32[1,2048]{1,0:T(1,128)}, f32[8,2048]{1,0:T(8,128)}) custom-call(bf16[4,144,2048]{2,1,0:T(8,128)(2,1)} %bitcast.7, bf16[4,144,2048]{2,1,0:T(8,128)(2,1)} %bitcast.8, bf16[3,64,256]{2,1,0:T(8,128)(2,1)} %bitcast.9, bf16[64,256]{1,0:T(8,128)(2,1)} %wo.1, ...), custom_call_target="tpu_custom_call" | custom-call | tf_op jit(solution)/shard_map/pallas_call | solution.py:691
  108.4 2.8 %shard_map.120 = (bf16[4,144,2048]{2,1,0:T(8,128)(2,1)}, f32[3,64,256]{2,1,0:T(8,128)}, f32[64,256]{1,0:T(8,128)}, f32[1,2048]{1,0:T(1,128)}, f32[8,2048]{1,0:T(8,128)}) custom-call(bf16[4,144,2048]{2,1,0:T(8,128)(2,1)} %get-tuple-element.15.refs_0_, f32[3,64,256]{2,1,0:T(8,128)} %get-tuple-element.16.refs_1_, f32[64,256]{1,0:T(8,128)} %get-tuple-element.17.refs_2_, ...), custom_call_target="tpu_custom_call" | custom-call | tf_op jit(solution)/shard_map/pallas_call | solution.py:721
